TPU v7x, 512 devices: a whole 4x8x8 slice. The times are simulated.
512 devices in a mesh: band: 128 (over y, z, core), lon: 4 (over x).
Axes of the slice: x: 4, y: 8, z: 8, core: 2. Of those that a mesh axis runs over, the one named last changes fastest.
Arguments:
- qu_values: float32 [2, 131072, 128], P(None, ('band', 'lon')), may hold values from -1.5 to 1.5
- tap_offsets: float32 [2, 131072, 128], P(None, ('band', 'lon')), may hold values from 0 to 1
- row_base: int32 [131072, 128], P(('band', 'lon')), may hold values from 0 to 8
- col_base: int32 [131072, 128], P(('band', 'lon')), may hold values from 0 to 120
- tile_of_block: int32 [131072], P(('band', 'lon')), may hold values from 0 to 63, as said below
- m_orders: int32 [1024], replicated, may hold values from 0 to 4095, as said below
Outputs:
- spectra: float32 [1024, 4, 4096], P(('band', 'lon'))
Inputs may be any that keep to these rules, and one draw needn't show every extreme that they name: `tile_of_block`: tiles of a band and longitude block are numbered row-major over (4) tile rows of 8192 // (4 * 128) tiles; the first and last tile rows lie in the neighbouring bands. Blocks of the first band never name the first tile row, blocks of the last band never the last. `m_orders`: entries 2k and 2k + 1 sum to 4095; all entries are distinct when 1024 <= 4096.
All inputs are finite; a program needn't handle non-finite values.
Results may differ from a plain program's by a relative error of at most 0.0001.
Values sent between devices are 32-bit elements; how exact they have to be, the bound alone decides.
A program may use at most 64 MiB of HBM per device.

v0:
```python
import math

import jax
import jax.numpy as jnp
from jax import lax
from jax.sharding import PartitionSpec as P

NPHI = 8192
ROWS_DEV = 32
TR = 16
TC = 128


def from_behind(value, axis, steps):
    count = lax.axis_size(axis)
    leading, last = (max(0, -steps), min(count, count - steps))
    return lax.ppermute(value, axis, [(source, source + steps) for source in range(leading, last)])


def tap_weights(base_index, fraction, extent):
    positions = jnp.arange(extent, dtype=jnp.int32)
    offsets = positions[None, None, :] - base_index[..., None]
    distance = offsets.astype(fraction.dtype) - 3.0 - fraction[..., None]
    inside = (offsets >= 0) & (offsets < 8)
    return jnp.where(inside, jnp.exp(-distance * distance / 8.0), 0.0)


def fourier_rows(orders, column_index, field_rows, weight):
    order_count = orders.shape[0]
    block_size = math.gcd(order_count, 256)

    def one_block(order_block):
        phase_index = order_block[:, None] * column_index[None, :] % NPHI
        angle_value = phase_index.astype(jnp.float32) * (2.0 * math.pi / NPHI)
        real_part = jnp.einsum(
            "frk,mk->mfr", field_rows, jnp.cos(angle_value), precision=lax.Precision.HIGHEST
        )
        imag_part = -jnp.einsum(
            "frk,mk->mfr", field_rows, jnp.sin(angle_value), precision=lax.Precision.HIGHEST
        )
        stacked = jnp.stack([real_part, imag_part], axis=2) * weight[None, None, None, :]
        return stacked.reshape(order_block.shape[0], -1)

    results = lax.map(one_block, orders.reshape(-1, block_size))
    return results.reshape(order_count, -1)


def body(qu_values, tap_offsets, row_base, col_base, tile_of_block, m_orders):
    band_count = lax.axis_size("band")
    lon_count = lax.axis_size("lon")
    band_index = lax.axis_index("band")
    lon_index = lax.axis_index("lon")
    columns = NPHI // lon_count
    tile_cols = columns // TC
    tile_rows = ROWS_DEV // TR + 2
    tile_count = tile_rows * tile_cols
    block_total = qu_values.shape[1]
    group_size = min(block_total, 64)

    def deposit(step_index, tile_totals):
        first_block = step_index * group_size
        values = lax.dynamic_slice_in_dim(qu_values, first_block, group_size, 1)
        fractions = lax.dynamic_slice_in_dim(tap_offsets, first_block, group_size, 1)
        row_taps = tap_weights(
            lax.dynamic_slice_in_dim(row_base, first_block, group_size, 0), fractions[0], TR
        )
        col_taps = tap_weights(
            lax.dynamic_slice_in_dim(col_base, first_block, group_size, 0), fractions[1], TC
        )
        tile_sums = jnp.einsum(
            "fgpr,gpc->gfrc",
            row_taps[None] * values[..., None],
            col_taps,
            precision=lax.Precision.HIGHEST,
        )
        targets = lax.dynamic_slice_in_dim(tile_of_block, first_block, group_size, 0)
        selector = (jnp.arange(tile_count, dtype=jnp.int32)[:, None] == targets[None, :]).astype(
            jnp.float32
        )
        return tile_totals + jnp.dot(
            selector, tile_sums.reshape(group_size, -1), precision=lax.Precision.HIGHEST
        )

    tile_totals = lax.fori_loop(
        0, block_total // group_size, deposit, jnp.zeros((tile_count, 2 * TR * TC), jnp.float32)
    )
    extended = (
        tile_totals.reshape(tile_rows, tile_cols, 2, TR, TC)
        .transpose(2, 0, 3, 1, 4)
        .reshape(2, tile_rows * TR, columns)
    )
    from_above = from_behind(extended[:, tile_rows * TR - TR :], "band", 1)
    from_below = from_behind(extended[:, :TR], "band", -1)
    own_rows = extended[:, TR : TR + ROWS_DEV]
    own_rows = own_rows.at[:, :TR].add(from_above).at[:, ROWS_DEV - TR :].add(from_below)
    total_rows = ROWS_DEV * band_count
    cycle_index = band_index * ROWS_DEV + jnp.arange(ROWS_DEV, dtype=jnp.int32)
    own_colatitude = math.pi * (cycle_index.astype(jnp.float32) + 0.5) / total_rows
    weight = math.pi * math.sqrt(2.0 / (total_rows * NPHI)) * jnp.sin(own_colatitude)
    per_device = m_orders.shape[0] // (band_count * lon_count)
    lon_orders = m_orders.reshape(band_count, lon_count, per_device).transpose(1, 0, 2).reshape(-1)
    column_index = lon_index * columns + jnp.arange(columns, dtype=jnp.int32)
    transformed = lax.psum_scatter(
        fourier_rows(lon_orders, column_index, own_rows, weight),
        "lon",
        scatter_dimension=0,
        tiled=True,
    )
    exchanged = lax.all_to_all(transformed, "band", split_axis=0, concat_axis=1, tiled=True)
    return (
        exchanged.reshape(per_device, band_count, 4, ROWS_DEV)
        .transpose(0, 2, 1, 3)
        .reshape(per_device, 4, total_rows)
    )


def solution(mesh):
    placed = (
        P(None, ("band", "lon"), None),
        P(None, ("band", "lon"), None),
        P(("band", "lon"), None),
        P(("band", "lon"), None),
        P(("band", "lon")),
        P(),
    )
    return jax.shard_map(
        body, mesh=mesh, in_specs=placed, out_specs=P(("band", "lon"), None, None), check_vma=False
    )
```

profile of v0, /device:TPU:1, one launch (start us, length us, event | category | flops | bytes accessed | tf_op | source)
XLA Modules:
  0.0 211.8 jit_solution(13344500508720533476)
XLA Ops:
  6.5 45.1 %while.33 = (s32[]{:T(128)}, f32[64,4096]{1,0:T(8,128)S(1)}, s32[256]{0:T(256)}, s32[256,128]{1,0:T(8,128)}, f32[2,256,128]{2,1,0:T(8,128)}, /*index=5*/f32[2,25...) while((s32[]{:T(128)}, f32[64,4096]{1,0:T(8,128)S(1)}, ...), condition=%wide.region_1.2_spmd.clone, body=%wide.region_0.1_spmd.clone.sunk | while | flops 617746432 | bytes 5968873 | solution.py:84
  9.3 6.8 %fusion.96 = f32[64,2,16,128]{3,2,1,0:T(8,128)S(1)} fusion(f32[64,128]{1,0:T(8,128)S(1)} %get-tuple-element.495, s32[64,128]{1,0:T(8,128)S(1)} %get-tuple-element.496, f32[2,64,128]{2,0,1:T(2,128)S(1)} %copy.40, f32[64,128,16]{1,2,0:T(8,128)S(1)} %fusion.95), kind=kOutput, calls=%fused_computation.39.clone.1 | convolution fusion | flops 414449664 | bytes 1703936 | tf_op jit(solution)/shard_map/while/body/eval_jaxpr/fgpr,gpc->gfrc/dot_general | solution.py:70
  16.1 1.7 convolution_add_fusion.2
  20.5 6.8 %fusion.96 = f32[64,2,16,128]{3,2,1,0:T(8,128)S(1)} fusion(f32[64,128]{1,0:T(8,128)S(1)} %get-tuple-element.495, s32[64,128]{1,0:T(8,128)S(1)} %get-tuple-element.496, f32[2,64,128]{2,0,1:T(2,128)S(1)} %copy.40, f32[64,128,16]{1,2,0:T(8,128)S(1)} %fusion.95), kind=kOutput, calls=%fused_computation.39.clone.1 | convolution fusion | flops 414449664 | bytes 1703936 | tf_op jit(solution)/shard_map/while/body/eval_jaxpr/fgpr,gpc->gfrc/dot_general | solution.py:70
  27.4 1.7 convolution_add_fusion.2
  31.8 6.8 %fusion.96 = f32[64,2,16,128]{3,2,1,0:T(8,128)S(1)} fusion(f32[64,128]{1,0:T(8,128)S(1)} %get-tuple-element.495, s32[64,128]{1,0:T(8,128)S(1)} %get-tuple-element.496, f32[2,64,128]{2,0,1:T(2,128)S(1)} %copy.40, f32[64,128,16]{1,2,0:T(8,128)S(1)} %fusion.95), kind=kOutput, calls=%fused_computation.39.clone.1 | convolution fusion | flops 414449664 | bytes 1703936 | tf_op jit(solution)/shard_map/while/body/eval_jaxpr/fgpr,gpc->gfrc/dot_general | solution.py:70
  38.7 1.7 convolution_add_fusion.2
  43.1 6.8 %fusion.96 = f32[64,2,16,128]{3,2,1,0:T(8,128)S(1)} fusion(f32[64,128]{1,0:T(8,128)S(1)} %get-tuple-element.495, s32[64,128]{1,0:T(8,128)S(1)} %get-tuple-element.496, f32[2,64,128]{2,0,1:T(2,128)S(1)} %copy.40, f32[64,128,16]{1,2,0:T(8,128)S(1)} %fusion.95), kind=kOutput, calls=%fused_computation.39.clone.1 | convolution fusion | flops 414449664 | bytes 1703936 | tf_op jit(solution)/shard_map/while/body/eval_jaxpr/fgpr,gpc->gfrc/dot_general | solution.py:70
  50.0 1.7 convolution_add_fusion.2
  52.7 5.4 %collective-permute-start = (f32[2,16,2048]{2,1,0:T(8,128)S(1)}, f32[2,16,2048]{2,1,0:T(8,128)S(1)}, u32[]{:S(2)}, u32[]{:S(2)}) collective-permute-start(f32[2,16,2048]{2,1,0:T(8,128)S(1)} %get-tuple-element.410), channel_id=1, source_target_pairs={{0,4},{4,8},{8,12},{12,16},{16,20},{20,24},{24,28},{28,32},{32,36}... | collective-permute-start | bytes 786440 | tf_op jit(solution)/shard_map/ppermute | solution.py:17
  58.1 4.7 %collective-permute-start.1 = (f32[2,16,2048]{2,1,0:T(8,128)S(1)}, f32[2,16,2048]{2,1,0:T(8,128)S(1)}, u32[]{:S(2)}, u32[]{:S(2)}) collective-permute-start(f32[2,16,2048]{2,1,0:T(8,128)S(1)} %get-tuple-element.409), channel_id=1, source_target_pairs={{4,0},{8,4},{12,8},{16,12},{20,16},{24,20},{28,24},{32,28},{36,32}... | collective-permute-start | bytes 786440 | tf_op jit(solution)/shard_map/ppermute | solution.py:17
  64.2 1.6 collective-permute-done.1
  65.8 80.8 %while.32 = (s32[]{:T(128)}, f32[4,256,128]{2,1,0:T(8,128)}, s32[4,256]{1,0:T(4,128)S(1)}, f32[2,32,2048]{2,1,0:T(8,128)S(1)}, s32[]{:T(128)}, /*index=5*/s32[]{:T(128)}, s32[]{:T(128)}) while((s32[]{:T(128)}, f32[4,256,128]{2,1,0:T(8,128)}, s32[4,256]{1,0:T(4,128)S(1)}, f32[2,32,2048]{2,1,0:T(8,128)S(1)}, s32[]{:T(128)}, ...), condition=%wide.region_3.4_spmd.clone, body=%wide.region_2.3_spmd.clone.sunk | while | flops 820070528 | bytes 2521945 | solution.py:44
  66.1 9.6 %fusion.90 = f32[256,2,1,32]{0,3,1,2:T(8,128)S(1)} fusion(f32[2,32,2048]{2,1,0:T(8,128)S(1)} %get-tuple-element.552, s32[2048]{0:T(1024)S(1)} %iota_add_fusion.2, s32[256]{0:T(256)S(1)} %bitcast.85), kind=kOutput, calls=%fused_computation.18.clone.1 | convolution fusion | flops 410009600 | bytes 599040 | tf_op jit(solution)/shard_map/while/body/eval_jaxpr/frk,mk->mfr/dot_general | solution.py:38
  75.6 9.5 %fusion.91 = f32[256,2,1,32]{0,3,1,2:T(8,128)S(1)} fusion(f32[2,32,2048]{2,1,0:T(8,128)S(1)} %get-tuple-element.552, s32[2048]{0:T(1024)S(1)} %iota_add_fusion.2, s32[256]{0:T(256)S(1)} %bitcast.86), kind=kOutput, calls=%fused_computation.16.clone.1 | convolution fusion | flops 409993216 | bytes 599040 | tf_op jit(solution)/shard_map/while/body/eval_jaxpr/frk,mk->mfr/dot_general | solution.py:35
  86.2 9.6 %fusion.90 = f32[256,2,1,32]{0,3,1,2:T(8,128)S(1)} fusion(f32[2,32,2048]{2,1,0:T(8,128)S(1)} %get-tuple-element.552, s32[2048]{0:T(1024)S(1)} %iota_add_fusion.2, s32[256]{0:T(256)S(1)} %bitcast.85), kind=kOutput, calls=%fused_computation.18.clone.1 | convolution fusion | flops 410009600 | bytes 599040 | tf_op jit(solution)/shard_map/while/body/eval_jaxpr/frk,mk->mfr/dot_general | solution.py:38
  95.8 9.5 %fusion.91 = f32[256,2,1,32]{0,3,1,2:T(8,128)S(1)} fusion(f32[2,32,2048]{2,1,0:T(8,128)S(1)} %get-tuple-element.552, s32[2048]{0:T(1024)S(1)} %iota_add_fusion.2, s32[256]{0:T(256)S(1)} %bitcast.86), kind=kOutput, calls=%fused_computation.16.clone.1 | convolution fusion | flops 409993216 | bytes 599040 | tf_op jit(solution)/shard_map/while/body/eval_jaxpr/frk,mk->mfr/dot_general | solution.py:35
  106.3 9.6 %fusion.90 = f32[256,2,1,32]{0,3,1,2:T(8,128)S(1)} fusion(f32[2,32,2048]{2,1,0:T(8,128)S(1)} %get-tuple-element.552, s32[2048]{0:T(1024)S(1)} %iota_add_fusion.2, s32[256]{0:T(256)S(1)} %bitcast.85), kind=kOutput, calls=%fused_computation.18.clone.1 | convolution fusion | flops 410009600 | bytes 599040 | tf_op jit(solution)/shard_map/while/body/eval_jaxpr/frk,mk->mfr/dot_general | solution.py:38
  115.9 9.5 %fusion.91 = f32[256,2,1,32]{0,3,1,2:T(8,128)S(1)} fusion(f32[2,32,2048]{2,1,0:T(8,128)S(1)} %get-tuple-element.552, s32[2048]{0:T(1024)S(1)} %iota_add_fusion.2, s32[256]{0:T(256)S(1)} %bitcast.86), kind=kOutput, calls=%fused_computation.16.clone.1 | convolution fusion | flops 409993216 | bytes 599040 | tf_op jit(solution)/shard_map/while/body/eval_jaxpr/frk,mk->mfr/dot_general | solution.py:35
  126.5 9.6 %fusion.90 = f32[256,2,1,32]{0,3,1,2:T(8,128)S(1)} fusion(f32[2,32,2048]{2,1,0:T(8,128)S(1)} %get-tuple-element.552, s32[2048]{0:T(1024)S(1)} %iota_add_fusion.2, s32[256]{0:T(256)S(1)} %bitcast.85), kind=kOutput, calls=%fused_computation.18.clone.1 | convolution fusion | flops 410009600 | bytes 599040 | tf_op jit(solution)/shard_map/while/body/eval_jaxpr/frk,mk->mfr/dot_general | solution.py:38
  136.0 9.5 %fusion.91 = f32[256,2,1,32]{0,3,1,2:T(8,128)S(1)} fusion(f32[2,32,2048]{2,1,0:T(8,128)S(1)} %get-tuple-element.552, s32[2048]{0:T(1024)S(1)} %iota_add_fusion.2, s32[256]{0:T(256)S(1)} %bitcast.86), kind=kOutput, calls=%fused_computation.16.clone.1 | convolution fusion | flops 409993216 | bytes 599040 | tf_op jit(solution)/shard_map/while/body/eval_jaxpr/frk,mk->mfr/dot_general | solution.py:35
  146.6 28.8 %reduce-scatter.2.cloned.1.call-done = f32[256,128]{1,0:T(8,128)} async-done(((f32[1024,128]{1,0:T(8,128)}), f32[256,128]{1,0:T(8,128)}) %reduce-scatter.2.cloned.1.call-update) | async-done | bytes 131088 | tf_op jit(solution)/shard_map/reduce_scatter | solution.py:103
  175.5 28.2 %all_to_all.16 = f32[128,2,128]{2,1,0:T(2,128)S(1)} all-to-all(f32[128,2,128]{2,1,0:T(2,128)} %bitcast.84), channel_id=1, replica_groups=mesh['band'=128,'lon'=4] {'band'}, dimensions={0} | all-to-all | bytes 262144 | tf_op jit(solution)/shard_map/all_to_all | solution.py:109
  204.0 0.9 reshape.159
  (91 shorter events, 17.9 us)
Async XLA Ops:
  6.5 168.9 %reduce-scatter.2.cloned.1.call-start = ((), (), s32[]{:S(2)}) async-start(), calls=%async_computation.2 | async-start | bytes 655360 | tf_op jit(solution)/shard_map/reduce_scatter | solution.py:103
  9.2 6.8 %copy-start.1 = (s32[256]{0:T(256)S(1)}, s32[256]{0:T(256)}, u32[]{:S(2)}) copy-start(s32[256]{0:T(256)} %get-tuple-element.525) | copy-start | bytes 3076 | tf_op jit(solution)/shard_map/while
  20.5 6.8 %copy-start.1 = (s32[256]{0:T(256)S(1)}, s32[256]{0:T(256)}, u32[]{:S(2)}) copy-start(s32[256]{0:T(256)} %get-tuple-element.525) | copy-start | bytes 3076 | tf_op jit(solution)/shard_map/while
  31.8 6.8 %copy-start.1 = (s32[256]{0:T(256)S(1)}, s32[256]{0:T(256)}, u32[]{:S(2)}) copy-start(s32[256]{0:T(256)} %get-tuple-element.525) | copy-start | bytes 3076 | tf_op jit(solution)/shard_map/while
  43.1 6.8 %copy-start.1 = (s32[256]{0:T(256)S(1)}, s32[256]{0:T(256)}, u32[]{:S(2)}) copy-start(s32[256]{0:T(256)} %get-tuple-element.525) | copy-start | bytes 3076 | tf_op jit(solution)/shard_map/while
  52.6 10.2 %copy-start = (s32[1024]{0:T(1024)S(1)}, s32[1024]{0:T(1024)}, u32[]{:S(2)}) copy-start(s32[1024]{0:T(1024)} %param.19) | copy-start | bytes 12292
  52.7 11.5 %collective-permute-start = (f32[2,16,2048]{2,1,0:T(8,128)S(1)}, f32[2,16,2048]{2,1,0:T(8,128)S(1)}, u32[]{:S(2)}, u32[]{:S(2)}) collective-permute-start(f32[2,16,2048]{2,1,0:T(8,128)S(1)} %get-tuple-element.410), channel_id=1, source_target_pairs={{0,4},{4,8},{8,12},{12,16},{16,20},{20,24},{24,28},{28,32},{32,36}... | collective-permute-start | bytes 786440 | tf_op jit(solution)/shard_map/ppermute | solution.py:17
  58.1 7.7 %collective-permute-start.1 = (f32[2,16,2048]{2,1,0:T(8,128)S(1)}, f32[2,16,2048]{2,1,0:T(8,128)S(1)}, u32[]{:S(2)}, u32[]{:S(2)}) collective-permute-start(f32[2,16,2048]{2,1,0:T(8,128)S(1)} %get-tuple-element.409), channel_id=1, source_target_pairs={{4,0},{8,4},{12,8},{16,12},{20,16},{24,20},{28,24},{32,28},{36,32}... | collective-permute-start | bytes 786440 | tf_op jit(solution)/shard_map/ppermute | solution.py:17
Sparse Core Ops, SparseCore 0:
  146.8 28.6 reduce-scatter.1
where the time goes:
time: 213 us; the launch traced here: 212 us
  matrix products  110 us (52%)
  waiting for transfers between devices  30.4 us (14%)
  blocking collectives  28.2 us (13%)
  local copies, waits for them, and re-layouts  17.2 us (8%)
  between operations  13.5 us (6%)
  starting transfers between devices  10.1 us (5%)
    dot_general x4, matrix products, one_block(): jnp.einsum('frk,mk->mfr', field_rows, jnp.sin(angle_value), precision=lax...  38.3 us
    dot_general x4, matrix products, one_block(): jnp.einsum('frk,mk->mfr', field_rows, jnp.cos(angle_value), precision=lax...  38.1 us
    reduce_scatter x1, waiting for transfers between devices, body(): lax.psum_scatter(fourier_rows(lon_orders, column_index, own_rows, weight)...  28.8 us
    all_to_all x1, blocking collectives, body(): lax.all_to_all(transformed, 'band', split_axis=0, concat_axis=1, tiled=True)  28.2 us
    dot_general x4, matrix products, deposit(): jnp.einsum('fgpr,gpc->gfrc', row_taps[None] * values[..., None], col_taps...  27.1 us
    ppermute x2, starting transfers between devices, from_behind(): lax.ppermute(value, axis, [(source, source + steps) for source in range(l...  10.1 us
    dot_general x4, matrix products, deposit(): jnp.dot(selector, tile_sums.reshape(group_size, -1), precision=lax.Precis...  6.69 us
  transfers between devices with their start and end apart: 3, of which 2 were waited for; matrix products, arithmetic and copies ran while one was open for 1% of the time, Pallas kernels for 0%

commit v1 on v0

v1 whole, which is shorter than its diff:
```python
import functools, math
import jax, jax.numpy as jnp
from jax import lax
from jax.experimental import pallas as pl
from jax.experimental.pallas import tpu as pltpu
from jax.sharding import PartitionSpec as P

NPHI = 8192
ROWS_DEV = 32
TR, TC = 16, 128
MESH = pl.DeviceIdType.MESH


TAP_SCALE = -math.log2(math.e) / 8.0


def split(x):
    high = x.astype(jnp.bfloat16)
    return high, (x - high.astype(jnp.float32)).astype(jnp.bfloat16)


def cos_sin(quarters):
    whole = jnp.floor(quarters + 0.5)
    angle = (quarters - whole) * (math.pi / 2.0)
    square = angle * angle
    sine = angle * (1.0 + square * (-1.0 / 6 + square * (1.0 / 120 + square * (-1.0 / 5040))))
    cosine = 1.0 + square * (-0.5 + square * (1.0 / 24 + square * (-1.0 / 720 + square * (1.0 / 40320))))
    quadrant = whole.astype(jnp.int32)
    swapped = (quadrant & 1) != 0
    first = jnp.where(swapped, sine, cosine)
    second = jnp.where(swapped, cosine, sine)
    first = jnp.where(((quadrant + 1) & 2) != 0, -first, first)
    second = jnp.where((quadrant & 2) != 0, -second, second)
    return first, second


def nt_dot(a, b):
    return lax.dot_general(a, b, (((1,), (1,)), ((), ())), preferred_element_type=jnp.float32)


def spectra_kernel(bands, lons, subs, tiles_ref, orders_ref, out_ref, halo, order_col, t_hi, t_lo, turn, spin,
                   g_hi, g_lo, part, arrived, total, landed,
                   halo_send, halo_recv, x_send, x_recv, a_send, a_recv):
    band = lax.axis_index("band")
    lon = lax.axis_index("lon")
    per_lon = 2 * bands
    above = lax.rem(band + bands - 1, bands)
    below = lax.rem(band + 1, bands)

    barrier = pltpu.get_barrier_semaphore()

    def greet(step, carry):
        pl.semaphore_signal(barrier, inc=1, device_id=(lax.rem(band + step, bands), lon), device_id_type=MESH)
        return carry

    lax.fori_loop(1, bands, greet, 0)
    for step in range(1, lons):
        pl.semaphore_signal(barrier, inc=1, device_id=(band, lax.rem(lon + step, lons)), device_id_type=MESH)
    pl.semaphore_wait(barrier, bands - 1 + lons - 1)

    upward = pltpu.make_async_remote_copy(
        src_ref=tiles_ref.at[pl.ds(0, 16)], dst_ref=halo.at[1], send_sem=halo_send.at[0], recv_sem=halo_recv.at[1],
        device_id=(above, lon), device_id_type=MESH)
    downward = pltpu.make_async_remote_copy(
        src_ref=tiles_ref.at[pl.ds(48, 16)], dst_ref=halo.at[0], send_sem=halo_send.at[1], recv_sem=halo_recv.at[0],
        device_id=(below, lon), device_id_type=MESH)
    upward.start()
    downward.start()

    lane = lax.broadcasted_iota(jnp.int32, (1, 128), 1)
    half = lane // 64
    for row in range(8):
        order_col[pl.ds(row * 128, 128), :] = jnp.transpose(
            jnp.broadcast_to(orders_ref[pl.ds(row, 1), :].astype(jnp.float32), (128, 128)))
    cycle = band * ROWS_DEV + ((lane // 32) % 2) * TR + lane % 16
    _, sine = cos_sin((cycle.astype(jnp.float32) + 0.5) * (1.0 / 2048))
    weight = sine * (math.pi * math.sqrt(2.0 / (bands * ROWS_DEV * NPHI)))
    low_columns = lane.astype(jnp.float32) * (1.0 / 2048)
    spin_phase = (half * 1024 + lon * 2048).astype(jnp.float32) * (1.0 / 2048)

    def table(step, carry):
        ell = step // 2
        place = step % 2
        m = order_col[pl.ds(2 * ell + place, 128, stride=8), :]
        rows = pl.ds(pl.multiple_of(place * 128, 128), 128)
        for side in range(2):
            c, s = cos_sin(m * (low_columns + side * (128.0 / 2048)))
            c_hi, c_lo = split(c)
            s_hi, s_lo = split(-s)
            cols = pl.ds(side * 128, 128)
            t_hi[ell, 0, rows, cols] = c_hi
            t_lo[ell, 0, rows, cols] = c_lo
            t_hi[ell, 1, rows, cols] = s_hi
            t_lo[ell, 1, rows, cols] = s_lo
        c, s = cos_sin(m * (256.0 / 2048))
        turn[ell, 0, rows, :] = c
        turn[ell, 1, rows, :] = -s
        eighth = (m.astype(jnp.int32) & 7).astype(jnp.float32)
        c, s = cos_sin(eighth * spin_phase)
        spin[ell, 0, rows, :] = c * weight
        spin[ell, 1, rows, :] = -s * weight
        return carry

    lax.fori_loop(0, 2 * lons, table, 0)

    upward.wait_recv()
    downward.wait_recv()

    for v in range(4):
        for h in range(2):
            for tr in range(2):
                place = v * 128 + h * 64 + tr * 32
                for k in range(2):
                    tile = 2 * (v + 4 * h) + k
                    value = tiles_ref[16 * (tr + 1) + tile] + halo[tr, tile]
                    hi, lo = split(value)
                    g_hi[pl.ds(place, 32), pl.ds(k * 128, 128)] = hi
                    g_lo[pl.ds(place, 32), pl.ds(k * 128, 128)] = lo

    is_real = lane < 64

    def transform(ell):
        for place in range(2):
            rows = pl.ds(place * 128, 128)
            cs = []
            for q in range(2):
                hi = t_hi[ell, q, rows, :]
                lo = t_lo[ell, q, rows, :]
                cs.append(nt_dot(hi, g_hi[...]) + nt_dot(hi, g_lo[...]) + nt_dot(lo, g_hi[...]))
            c, s = cs
            wr = turn[ell, 0, rows, :]
            wi = turn[ell, 1, rows, :]
            re, im = c[:, 384:], s[:, 384:]
            for v in (2, 1, 0):
                re, im = (re * wr - im * wi + c[:, v * 128:v * 128 + 128],
                          re * wi + im * wr + s[:, v * 128:v * 128 + 128])
            pr = spin[ell, 0, rows, :]
            pi = spin[ell, 1, rows, :]
            zr = re * pr - im * pi
            zi = re * pi + im * pr
            zr = zr + pltpu.roll(zr, 64, 1)
            zi = zi + pltpu.roll(zi, 64, 1)
            part[ell, pl.ds(place, 128, stride=2), :] = jnp.where(is_real, zr, zi)

    per_sub = per_lon // subs
    quarter = band // (bands // subs)

    def sub_rows(sub):
        return pl.ds(pl.multiple_of(lax.rem(quarter + sub, subs) * per_sub, per_sub), per_sub)

    def over_lon(ell, source, sub):
        return pltpu.make_async_remote_copy(
            src_ref=part.at[ell, sub_rows(sub), :], dst_ref=arrived.at[source, sub_rows(sub), :],
            send_sem=x_send.at[ell, sub], recv_sem=x_recv.at[source, sub],
            device_id=(band, ell), device_id_type=MESH)

    def send_part(step, carry):
        ell = lax.rem(lon + step, lons)
        transform(ell)
        for sub in range(subs):
            over_lon(ell, lon, sub).start()
        return carry

    lax.fori_loop(1, lons, send_part, 0)
    transform(lon)

    for sub in range(subs):
        rows = sub_rows(sub)
        value = part[lon, rows, :]
        for step in range(1, lons):
            source = lax.rem(lon + step, lons)
            pltpu.make_async_remote_copy(
                src_ref=arrived.at[source, rows, :], dst_ref=arrived.at[source, rows, :],
                send_sem=x_send.at[source, sub], recv_sem=x_recv.at[source, sub],
                device_id=(band, source), device_id_type=MESH).wait_recv()
            value = value + arrived[source, rows, :]
        total[rows, :] = value
        first = lax.rem(quarter + sub, subs) * (bands // subs)

        def send_total(step, carry):
            target = first + step

            @pl.when(target != band)
            def _():
                pltpu.make_async_remote_copy(
                    src_ref=total.at[pl.ds(2 * target, 2), :], dst_ref=landed.at[pl.ds(2 * band, 2), :],
                    send_sem=a_send, recv_sem=a_recv, device_id=(target, lon), device_id_type=MESH).start()
            return carry

        lax.fori_loop(0, bands // subs, send_total, 0)

    own = pltpu.make_async_copy(total.at[pl.ds(2 * band, 2), :], landed.at[pl.ds(2 * band, 2), :], a_recv)
    own.start()
    pltpu.make_async_copy(landed, landed, a_recv).wait()

    lanes = lax.broadcasted_iota(jnp.int32, (bands // 4, 128), 1)
    for i in range(2):
        for f in range(2):
            for reim in range(2):
                value = jnp.zeros((bands // 4, 128), jnp.float32)
                for q in range(4):
                    x = landed[pl.ds(2 * q + i, bands // 4, stride=8), :]
                    for tr in range(2):
                        source = reim * 4 + tr * 2 + f
                        target = 2 * q + tr
                        moved = x if source == target else pltpu.roll(x, ((target - source) % 8) * 16, 1)
                        value = jnp.where(lanes // 16 == target, moved, value)
                for j in range(bands // 4):
                    out_ref[i, pl.ds(2 * f + reim, 1), pl.ds(j * 128, 128)] = value[j:j + 1, :]

    upward.wait_send()
    downward.wait_send()
    for step in range(1, lons):
        ell = lax.rem(lon + step, lons)
        for sub in range(subs):
            over_lon(ell, lon, sub).wait_send()
    others = pl.ds(0, per_lon - 2)
    pltpu.make_async_copy(total.at[others], total.at[others], a_send).wait()


def spectra(tiles, orders, bands, lons, subs=4, local=False):
    V = pl.BlockSpec(memory_space=pltpu.VMEM)
    f32, bf16 = jnp.float32, jnp.bfloat16
    return pl.pallas_call(
        functools.partial(spectra_kernel, bands, lons, subs),
        out_shape=jax.ShapeDtypeStruct((2, 4, bands * ROWS_DEV), f32),
        in_specs=[V, V],
        out_specs=V,
        scratch_shapes=[
            pltpu.VMEM((2, 16, 32, 128), f32),
            pltpu.VMEM((1024, 128), f32),
            pltpu.VMEM((lons, 2, 256, 256), bf16),
            pltpu.VMEM((lons, 2, 256, 256), bf16),
            pltpu.VMEM((lons, 2, 256, 128), f32),
            pltpu.VMEM((lons, 2, 256, 128), f32),
            pltpu.VMEM((512, 256), bf16),
            pltpu.VMEM((512, 256), bf16),
            pltpu.VMEM((lons, 256, 128), f32),
            pltpu.VMEM((lons, 256, 128), f32),
            pltpu.VMEM((256, 128), f32),
            pltpu.VMEM((256, 128), f32),
            pltpu.SemaphoreType.DMA((2,)),
            pltpu.SemaphoreType.DMA((2,)),
            pltpu.SemaphoreType.DMA((lons, subs)),
            pltpu.SemaphoreType.DMA((lons, subs)),
            pltpu.SemaphoreType.DMA,
            pltpu.SemaphoreType.DMA,
        ],
        compiler_params=pltpu.CompilerParams(collective_id=0, has_side_effects=True, vmem_limit_bytes=40 * 1024 * 1024),
    )(tiles, orders)


def deposit_kernel(unroll, tile_ref, qu_ref, off_ref, rb_ref, cb_ref, tiles_ref):
    tiles_ref[...] = jnp.zeros_like(tiles_ref)
    pos = lax.broadcasted_iota(jnp.int32, (16, 128), 0)

    def one(n):
        row = pl.ds(n, 1)
        cb = cb_ref[row, :]
        col_o = (pos - cb) & 15
        d = col_o.astype(jnp.float32) - (off_ref[1, row, :] + 3.0)
        v = jnp.exp2(d * d * TAP_SCALE)
        v_hi, v_lo = split(v)
        group = jnp.where(col_o < 8, cb + col_o - pos, -16).astype(jnp.bfloat16)
        zero = jnp.zeros((16, 128), jnp.bfloat16)
        hi, lo = [], []
        for ch in range(8):
            m = group == jnp.bfloat16(16 * ch)
            hi.append(jnp.where(m, v_hi, zero))
            lo.append(jnp.where(m, v_lo, zero))
        cols = jnp.concatenate([jnp.concatenate(hi, 0), jnp.concatenate(lo, 0)], 1)
        row_o = (pos - rb_ref[row, :]) & 15
        e = row_o.astype(jnp.float32) - (off_ref[0, row, :] + 3.0)
        a = jnp.where(row_o < 8, jnp.exp2(e * e * TAP_SCALE), 0.0)
        q_hi, q_lo = split(a * qu_ref[0, row, :])
        u_hi, u_lo = split(a * qu_ref[1, row, :])
        half = jnp.concatenate([q_hi, u_hi, q_lo, u_lo], 0)
        rows = jnp.concatenate([half, half], 1)
        out = lax.dot_general(rows, cols, (((1,), (1,)), ((), ())), preferred_element_type=jnp.float32)
        return out[:32] + out[32:]

    def step(i, carry):
        outs = [(tile_ref[i * unroll + j], one(i * unroll + j)) for j in range(unroll)]
        for t, o in outs:
            tiles_ref[t] += o
        return carry

    lax.fori_loop(0, 256 // unroll, step, 0)

def deposit(qu, off, rb, cb, tile, unroll=8):
    V = pl.BlockSpec(memory_space=pltpu.VMEM)
    return pl.pallas_call(
        functools.partial(deposit_kernel, unroll),
        out_shape=jax.ShapeDtypeStruct((64, 32, 128), jnp.float32),
        in_specs=[pl.BlockSpec(memory_space=pltpu.SMEM), V, V, V, V],
        out_specs=V,
    )(tile, qu, off, rb, cb)


def body(qu_values, tap_offsets, row_base, col_base, tile_of_block, m_orders):
    bands = lax.axis_size("band")
    lons = lax.axis_size("lon")
    tiles = deposit(qu_values, tap_offsets, row_base, col_base, tile_of_block, 32)
    return spectra(tiles, m_orders.reshape(8, 128), bands, lons)


def solution(mesh):
    placed = (
        P(None, ("band", "lon"), None),
        P(None, ("band", "lon"), None),
        P(("band", "lon"), None),
        P(("band", "lon"), None),
        P(("band", "lon")),
        P(),
    )
    return jax.shard_map(
        body, mesh=mesh, in_specs=placed, out_specs=P(("band", "lon"), None, None), check_vma=False
    )
```

time: 213 us -> 50.9 us (0.24)
  matrix products: 110 us -> 0 us
  Pallas kernels: 0 us -> 48.8 us
  waiting for transfers between devices: 30.4 us -> 0 us
  blocking collectives: 28.2 us -> 0 us
  local copies, waits for them, and re-layouts: 17.2 us -> 1.89 us
  between operations: 13.5 us -> 0.01 us
  starting transfers between devices: 10.1 us -> 0 us
    dot_general x16 -> x0, matrix products: 110 us -> none  [the longest x4 38.3 us: one_block(): jnp.einsum('frk,mk->mfr', field_rows, jnp.sin(angle_value), precision=lax...]
    pallas_call x0 -> x2, Pallas kernels: none -> 48.8 us  [the longest x1 39.8 us: spectra(): pl.pallas_call(functools.partial(spectra_kernel, bands, lons, subs), out_...]
    reduce_scatter x1 -> x0, waiting for transfers between devices: 28.8 us -> none  [body(): lax.psum_scatter(fourier_rows(lon_orders, column_index, own_rows, weight)...]
    all_to_all x1 -> x0, blocking collectives: 28.2 us -> none  [body(): lax.all_to_all(transformed, 'band', split_axis=0, concat_axis=1, tiled=True)]
    ppermute x2 -> x0, starting transfers between devices: 10.1 us -> none  [from_behind(): lax.ppermute(value, axis, [(source, source + steps) for source in range(l...]
    dynamic_slice x20 -> x0, local copies, waits for them, and re-layouts: 7.11 us -> none  [the longest x8 3.63 us: deposit(): values = lax.dynamic_slice_in_dim(qu_values, first_block, group_size, 1)]
    sub x4 -> x0, local copies, waits for them, and re-layouts: 3.12 us -> none  [tap_weights(): distance = offsets.astype(fraction.dtype) - 3.0 - fraction[..., None]]
    dynamic_update_slice x8 -> x0, local copies, waits for them, and re-layouts: 3 us -> none  [fourier_rows(): results = lax.map(one_block, orders.reshape(-1, block_size))]
  transfers between devices with their start and end apart: 3 -> 0, of which waited for: 2 -> 0; matrix products, arithmetic and copies ran while one was open for 1% -> 0% of each run, Pallas kernels for 0% -> 0%
where the time goes in v1:
time: 50.9 us; the launch traced here: 50.7 us
  Pallas kernels  48.8 us (96%)
  local copies, waits for them, and re-layouts  1.89 us (4%)
    pallas_call x1, Pallas kernels, spectra(): pl.pallas_call(functools.partial(spectra_kernel, bands, lons, subs), out_...  39.8 us
    pallas_call x1, Pallas kernels, deposit(): pl.pallas_call(functools.partial(deposit_kernel, unroll), out_shape=jax.S...  9.06 us
    unnamed x5, local copies, waits for them, and re-layouts  1.89 us

profile of v1, /device:TPU:1, one launch (start us, length us, event | category | flops | bytes accessed | tf_op | source)
XLA Modules:
  0.0 50.7 jit_solution(9614713384495686504)
XLA Ops:
  0.0 0.0 copy-start.1
  0.0 9.1 %shard_map.64.tiles_ref = f32[64,32,128]{2,1,0:T(8,128)} custom-call(s32[256]{0:T(256)} %tile_ref.1, f32[2,256,128]{2,1,0:T(8,128)} %qu_ref.1, f32[2,256,128]{2,1,0:T(8,128)} %off_ref.1, s32[256,128]{1,0:T(8,128)} %rb_ref.1, s32[256,128]{1,0:T(8,128)} %cb_ref.1), custom_call_target="tpu_custom_call" | custom-call | tf_op jit(solution)/shard_map/pallas_call | solution.py:292
  9.1 0.0 copy-done.1
  9.1 0.0 copy-start
  9.1 1.2 %copy-done = f32[64,32,128]{2,1,0:T(8,128)S(1)} copy-done((f32[64,32,128]{2,1,0:T(8,128)S(1)}, f32[64,32,128]{2,1,0:T(8,128)}, u32[]{:S(2)}) %copy-start) | copy-done | bytes 1048600
  10.3 39.8 %shard_map.65 = f32[2,4,4096]{2,1,0:T(4,128)S(1)} custom-call(f32[64,32,128]{2,1,0:T(8,128)S(1)} %copy-done, s32[8,128]{1,0:T(8,128)S(1)} %bitcast.1), custom_call_target="tpu_custom_call" | custom-call | tf_op jit(solution)/shard_map/pallas_call | solution.py:224
  50.1 0.7 %copy.8 = f32[2,4,4096]{2,1,0:T(4,128)} copy(f32[2,4,4096]{2,1,0:T(4,128)S(1)} %shard_map.65) | data formatting | bytes 262144
Async XLA Ops:
  0.0 9.1 %copy-start.1 = (s32[1024]{0:T(1024)S(1)}, s32[1024]{0:T(1024)}, u32[]{:S(2)}) copy-start(s32[1024]{0:T(1024)} %param.11) | copy-start | bytes 12292
  9.1 1.2 %copy-start = (f32[64,32,128]{2,1,0:T(8,128)S(1)}, f32[64,32,128]{2,1,0:T(8,128)}, u32[]{:S(2)}) copy-start(f32[64,32,128]{2,1,0:T(8,128)} %shard_map.64.tiles_ref) | copy-start | bytes 3145732

commit v2 on v1

--- a/solution.py
+++ b/solution.py
@@ -38,12 +38,16 @@
     return lax.dot_general(a, b, (((1,), (1,)), ((), ())), preferred_element_type=jnp.float32)
 
 
-def spectra_kernel(bands, lons, subs, tiles_ref, orders_ref, out_ref, halo, order_col, t_hi, t_lo, turn, spin,
+def spectra_kernel(bands, lons, subs, lag, tiles_ref, orders_ref, out_ref, halo, order_col, t_hi, t_lo, turn, spin,
                    g_hi, g_lo, part, arrived, total, landed,
                    halo_send, halo_recv, x_send, x_recv, a_send, a_recv):
     band = lax.axis_index("band")
     lon = lax.axis_index("lon")
     per_lon = 2 * bands
+    run = bands // subs
+    per_sub = 2 * run
+    per_group = per_sub * lons
+    quarter = band // run
     above = lax.rem(band + bands - 1, bands)
     below = lax.rem(band + 1, bands)
 
@@ -79,29 +83,30 @@
     spin_phase = (half * 1024 + lon * 2048).astype(jnp.float32) * (1.0 / 2048)
 
     def table(step, carry):
-        ell = step // 2
-        place = step % 2
-        m = order_col[pl.ds(2 * ell + place, 128, stride=8), :]
-        rows = pl.ds(pl.multiple_of(place * 128, 128), 128)
+        group = step // lons
+        ell = lax.rem(step, lons)
+        first = group * per_group + 2 * ell
+        m = jnp.concatenate([order_col[pl.ds(first + place, run, stride=2 * lons), :] for place in range(2)], 0)
+        rows = pl.ds(pl.multiple_of(ell * 2 * run, 2 * run), 2 * run)
         for side in range(2):
             c, s = cos_sin(m * (low_columns + side * (128.0 / 2048)))
             c_hi, c_lo = split(c)
             s_hi, s_lo = split(-s)
             cols = pl.ds(side * 128, 128)
-            t_hi[ell, 0, rows, cols] = c_hi
-            t_lo[ell, 0, rows, cols] = c_lo
-            t_hi[ell, 1, rows, cols] = s_hi
-            t_lo[ell, 1, rows, cols] = s_lo
+            t_hi[group, 0, rows, cols] = c_hi
+            t_lo[group, 0, rows, cols] = c_lo
+            t_hi[group, 1, rows, cols] = s_hi
+            t_lo[group, 1, rows, cols] = s_lo
         c, s = cos_sin(m * (256.0 / 2048))
-        turn[ell, 0, rows, :] = c
-        turn[ell, 1, rows, :] = -s
+        turn[group, 0, rows, :] = c
+        turn[group, 1, rows, :] = -s
         eighth = (m.astype(jnp.int32) & 7).astype(jnp.float32)
         c, s = cos_sin(eighth * spin_phase)
-        spin[ell, 0, rows, :] = c * weight
-        spin[ell, 1, rows, :] = -s * weight
-        return carry
-
-    lax.fori_loop(0, 2 * lons, table, 0)
+        spin[group, 0, rows, :] = c * weight
+        spin[group, 1, rows, :] = -s * weight
+        return carry
+
+    lax.fori_loop(0, subs * lons, table, 0)
 
     upward.wait_recv()
     downward.wait_recv()
@@ -119,66 +124,57 @@
 
     is_real = lane < 64
 
-    def transform(ell):
-        for place in range(2):
-            rows = pl.ds(place * 128, 128)
+    def transform(group):
+        for side in range(2):
+            rows = pl.ds(side * 128, 128)
             cs = []
             for q in range(2):
-                hi = t_hi[ell, q, rows, :]
-                lo = t_lo[ell, q, rows, :]
+                hi = t_hi[group, q, rows, :]
+                lo = t_lo[group, q, rows, :]
                 cs.append(nt_dot(hi, g_hi[...]) + nt_dot(hi, g_lo[...]) + nt_dot(lo, g_hi[...]))
             c, s = cs
-            wr = turn[ell, 0, rows, :]
-            wi = turn[ell, 1, rows, :]
+            wr = turn[group, 0, rows, :]
+            wi = turn[group, 1, rows, :]
             re, im = c[:, 384:], s[:, 384:]
             for v in (2, 1, 0):
                 re, im = (re * wr - im * wi + c[:, v * 128:v * 128 + 128],
                           re * wi + im * wr + s[:, v * 128:v * 128 + 128])
-            pr = spin[ell, 0, rows, :]
-            pi = spin[ell, 1, rows, :]
+            pr = spin[group, 0, rows, :]
+            pi = spin[group, 1, rows, :]
             zr = re * pr - im * pi
             zi = re * pi + im * pr
             zr = zr + pltpu.roll(zr, 64, 1)
             zi = zi + pltpu.roll(zi, 64, 1)
-            part[ell, pl.ds(place, 128, stride=2), :] = jnp.where(is_real, zr, zi)
-
-    per_sub = per_lon // subs
-    quarter = band // (bands // subs)
-
-    def sub_rows(sub):
-        return pl.ds(pl.multiple_of(lax.rem(quarter + sub, subs) * per_sub, per_sub), per_sub)
-
-    def over_lon(ell, source, sub):
+            z = jnp.where(is_real, zr, zi)
+            for k in range(128 // run):
+                ell, place = divmod(side * (128 // run) + k, 2)
+                part[group, ell, pl.ds(place, run, stride=2), :] = z[k * run:(k + 1) * run]
+
+    def over_lon(step, group, sub):
+        ell = lax.rem(lon + step, lons)
         return pltpu.make_async_remote_copy(
-            src_ref=part.at[ell, sub_rows(sub), :], dst_ref=arrived.at[source, sub_rows(sub), :],
-            send_sem=x_send.at[ell, sub], recv_sem=x_recv.at[source, sub],
+            src_ref=part.at[group, ell], dst_ref=arrived.at[group, lons - step],
+            send_sem=x_send.at[step, sub], recv_sem=x_recv.at[lons - step, sub],
             device_id=(band, ell), device_id_type=MESH)
 
-    def send_part(step, carry):
-        ell = lax.rem(lon + step, lons)
-        transform(ell)
-        for sub in range(subs):
-            over_lon(ell, lon, sub).start()
-        return carry
-
-    lax.fori_loop(1, lons, send_part, 0)
-    transform(lon)
-
-    for sub in range(subs):
-        rows = sub_rows(sub)
-        value = part[lon, rows, :]
+    def send_part(sub, carry):
+        group = lax.rem(quarter + sub, subs)
+        transform(group)
+        for step in (2, 1, 3):
+            over_lon(step, group, sub).start()
+        return carry
+
+    def send_total(sub, carry):
+        group = lax.rem(quarter + sub, subs)
+        value = part[group, lon]
         for step in range(1, lons):
-            source = lax.rem(lon + step, lons)
-            pltpu.make_async_remote_copy(
-                src_ref=arrived.at[source, rows, :], dst_ref=arrived.at[source, rows, :],
-                send_sem=x_send.at[source, sub], recv_sem=x_recv.at[source, sub],
-                device_id=(band, source), device_id_type=MESH).wait_recv()
-            value = value + arrived[source, rows, :]
+            over_lon(step, group, sub).wait_recv()
+            value = value + arrived[group, lons - step]
+        rows = pl.ds(pl.multiple_of(group * per_sub, per_sub), per_sub)
         total[rows, :] = value
-        first = lax.rem(quarter + sub, subs) * (bands // subs)
-
-        def send_total(step, carry):
-            target = first + step
+
+        def send_one(step, carry):
+            target = group * run + lax.rem(band + step, run)
 
             @pl.when(target != band)
             def _():
@@ -187,7 +183,19 @@
                     send_sem=a_send, recv_sem=a_recv, device_id=(target, lon), device_id_type=MESH).start()
             return carry
 
-        lax.fori_loop(0, bands // subs, send_total, 0)
+        return lax.fori_loop(0, run, send_one, carry)
+
+    def pipeline(sub, carry):
+        @pl.when(sub < subs)
+        def _():
+            send_part(sub, 0)
+
+        @pl.when(sub >= lag)
+        def _():
+            send_total(sub - lag, 0)
+        return carry
+
+    lax.fori_loop(0, subs + lag, pipeline, 0)
 
     own = pltpu.make_async_copy(total.at[pl.ds(2 * band, 2), :], landed.at[pl.ds(2 * band, 2), :], a_recv)
     own.start()
@@ -210,33 +218,32 @@
 
     upward.wait_send()
     downward.wait_send()
-    for step in range(1, lons):
-        ell = lax.rem(lon + step, lons)
-        for sub in range(subs):
-            over_lon(ell, lon, sub).wait_send()
+    for sub in range(subs):
+        for step in range(1, lons):
+            over_lon(step, lax.rem(quarter + sub, subs), sub).wait_send()
     others = pl.ds(0, per_lon - 2)
     pltpu.make_async_copy(total.at[others], total.at[others], a_send).wait()
 
 
-def spectra(tiles, orders, bands, lons, subs=4, local=False):
+def spectra(tiles, orders, bands, lons, subs=4, lag=2):
     V = pl.BlockSpec(memory_space=pltpu.VMEM)
     f32, bf16 = jnp.float32, jnp.bfloat16
     return pl.pallas_call(
-        functools.partial(spectra_kernel, bands, lons, subs),
+        functools.partial(spectra_kernel, bands, lons, subs, lag),
         out_shape=jax.ShapeDtypeStruct((2, 4, bands * ROWS_DEV), f32),
         in_specs=[V, V],
         out_specs=V,
         scratch_shapes=[
             pltpu.VMEM((2, 16, 32, 128), f32),
             pltpu.VMEM((1024, 128), f32),
-            pltpu.VMEM((lons, 2, 256, 256), bf16),
-            pltpu.VMEM((lons, 2, 256, 256), bf16),
-            pltpu.VMEM((lons, 2, 256, 128), f32),
-            pltpu.VMEM((lons, 2, 256, 128), f32),
+            pltpu.VMEM((subs, 2, 256, 256), bf16),
+            pltpu.VMEM((subs, 2, 256, 256), bf16),
+            pltpu.VMEM((subs, 2, 256, 128), f32),
+            pltpu.VMEM((subs, 2, 256, 128), f32),
             pltpu.VMEM((512, 256), bf16),
             pltpu.VMEM((512, 256), bf16),
-            pltpu.VMEM((lons, 256, 128), f32),
-            pltpu.VMEM((lons, 256, 128), f32),
+            pltpu.VMEM((subs, lons, 256 // subs, 128), f32),
+            pltpu.VMEM((subs, lons, 256 // subs, 128), f32),
             pltpu.VMEM((256, 128), f32),
             pltpu.VMEM((256, 128), f32),
             pltpu.SemaphoreType.DMA((2,)),
@@ -291,7 +298,7 @@
     V = pl.BlockSpec(memory_space=pltpu.VMEM)
     return pl.pallas_call(
         functools.partial(deposit_kernel, unroll),
-        out_shape=jax.ShapeDtypeStruct((64, 32, 128), jnp.float32),
+        out_shape=pltpu.VMEM((64, 32, 128), jnp.float32),
         in_specs=[pl.BlockSpec(memory_space=pltpu.SMEM), V, V, V, V],
         out_specs=V,
     )(tile, qu, off, rb, cb)

time: 50.9 us -> 50.5 us (level)
  local copies, waits for them, and re-layouts: 1.89 us -> 0.66 us
  Pallas kernels: 48.8 us -> 49.7 us
    unnamed x5 -> x3, local copies, waits for them, and re-layouts: 1.89 us -> 0.66 us
    pallas_call x2, Pallas kernels: 48.8 us -> 49.7 us  [the longest x1 41.6 us: spectra(): pl.pallas_call(functools.partial(spectra_kernel, bands, lons, subs, lag),...]
where the time goes in v2:
time: 50.5 us; the launch traced here: 50.4 us
  Pallas kernels  49.7 us (98%)
  local copies, waits for them, and re-layouts  0.66 us (1%)
    pallas_call x1, Pallas kernels, spectra(): pl.pallas_call(functools.partial(spectra_kernel, bands, lons, subs, lag),...  41.6 us
    pallas_call x1, Pallas kernels, deposit(): pl.pallas_call(functools.partial(deposit_kernel, unroll), out_shape=pltpu...  8.08 us

profile of v2, /device:TPU:1, one launch (start us, length us, event | category | flops | bytes accessed | tf_op | source)
XLA Modules:
  0.0 50.4 jit_solution(15509499814775139107)
XLA Ops:
  0.0 0.0 copy-start
  0.0 8.1 %shard_map.64.tiles_ref = f32[64,32,128]{2,1,0:T(8,128)S(1)} custom-call(s32[256]{0:T(256)} %tile_ref.1, f32[2,256,128]{2,1,0:T(8,128)} %qu_ref.1, f32[2,256,128]{2,1,0:T(8,128)} %off_ref.1, s32[256,128]{1,0:T(8,128)} %rb_ref.1, s32[256,128]{1,0:T(8,128)} %cb_ref.1), custom_call_target="tpu_custom_call" | custom-call | tf_op jit(solution)/shard_map/pallas_call | solution.py:299
  8.1 0.0 copy-done
  8.1 41.6 %shard_map.65 = f32[2,4,4096]{2,1,0:T(4,128)S(1)} custom-call(f32[64,32,128]{2,1,0:T(8,128)S(1)} %shard_map.64.tiles_ref, s32[8,128]{1,0:T(8,128)S(1)} %bitcast.1), custom_call_target="tpu_custom_call" | custom-call | tf_op jit(solution)/shard_map/pallas_call | solution.py:231
  49.7 0.7 %copy.8 = f32[2,4,4096]{2,1,0:T(4,128)} copy(f32[2,4,4096]{2,1,0:T(4,128)S(1)} %shard_map.65) | data formatting | bytes 262144
Async XLA Ops:
  0.0 8.1 %copy-start = (s32[1024]{0:T(1024)S(1)}, s32[1024]{0:T(1024)}, u32[]{:S(2)}) copy-start(s32[1024]{0:T(1024)} %param.11) | copy-start | bytes 12292

commit v3 on v2

--- a/solution.py
+++ b/solution.py
@@ -9,8 +9,6 @@
 ROWS_DEV = 32
 TR, TC = 16, 128
 MESH = pl.DeviceIdType.MESH
-
-
 TAP_SCALE = -math.log2(math.e) / 8.0
 
 
@@ -38,35 +36,87 @@
     return lax.dot_general(a, b, (((1,), (1,)), ((), ())), preferred_element_type=jnp.float32)
 
 
-def spectra_kernel(bands, lons, subs, lag, tiles_ref, orders_ref, out_ref, halo, order_col, t_hi, t_lo, turn, spin,
-                   g_hi, g_lo, part, arrived, total, landed,
+def spectra_kernel(bands, lons, subs, lag, unroll, target_ref, qu_ref, off_ref, rb_ref, cb_ref, orders_ref, out_ref,
+                   block_sums, tiles, halo, order_col, t_hi, t_lo, turn, spin, g_hi, g_lo, part, arrived, total, landed,
                    halo_send, halo_recv, x_send, x_recv, a_send, a_recv):
     band = lax.axis_index("band")
     lon = lax.axis_index("lon")
-    per_lon = 2 * bands
     run = bands // subs
     per_sub = 2 * run
     per_group = per_sub * lons
+    per_lon = 2 * bands
     quarter = band // run
     above = lax.rem(band + bands - 1, bands)
     below = lax.rem(band + 1, bands)
+    blocks = rb_ref.shape[0]
 
     barrier = pltpu.get_barrier_semaphore()
-
-    def greet(step, carry):
-        pl.semaphore_signal(barrier, inc=1, device_id=(lax.rem(band + step, bands), lon), device_id_type=MESH)
-        return carry
-
-    lax.fori_loop(1, bands, greet, 0)
     for step in range(1, lons):
         pl.semaphore_signal(barrier, inc=1, device_id=(band, lax.rem(lon + step, lons)), device_id_type=MESH)
+
+    pos = lax.broadcasted_iota(jnp.int32, (TR, 128), 0)
+
+    def block_tile(n):
+        row = pl.ds(n, 1)
+        cb = cb_ref[row, :]
+        col_o = (pos - cb) & 15
+        d = col_o.astype(jnp.float32) - (off_ref[1, row, :] + 3.0)
+        v_hi, v_lo = split(jnp.exp2(d * d * TAP_SCALE))
+        group = jnp.where(col_o < 8, cb + col_o - pos, -16).astype(jnp.bfloat16)
+        zero = jnp.zeros((TR, 128), jnp.bfloat16)
+        hi, lo = [], []
+        for sixteen in range(TC // 16):
+            here = group == jnp.bfloat16(16 * sixteen)
+            hi.append(jnp.where(here, v_hi, zero))
+            lo.append(jnp.where(here, v_lo, zero))
+        cols = jnp.concatenate([jnp.concatenate(hi, 0), jnp.concatenate(lo, 0)], 1)
+        row_o = (pos - rb_ref[row, :]) & 15
+        e = row_o.astype(jnp.float32) - (off_ref[0, row, :] + 3.0)
+        a = jnp.where(row_o < 8, jnp.exp2(e * e * TAP_SCALE), 0.0)
+        q_hi, q_lo = split(a * qu_ref[0, row, :])
+        u_hi, u_lo = split(a * qu_ref[1, row, :])
+        half = jnp.concatenate([q_hi, u_hi, q_lo, u_lo], 0)
+        out = nt_dot(jnp.concatenate([half, half], 1), cols)
+        return out[:2 * TR] + out[2 * TR:]
+
+    greets = bands * unroll // blocks
+
+    def deposit(i, carry):
+        for j in range(greets):
+            step = i * greets + j
+
+            @pl.when(step > 0)
+            def _():
+                pl.semaphore_signal(barrier, inc=1, device_id=(lax.rem(band + step, bands), lon), device_id_type=MESH)
+
+        for j in range(unroll):
+            n = i * unroll + j
+            block_sums[pl.ds(n, 2 * TR, stride=blocks), :] = block_tile(n)
+        return carry
+
+    lax.fori_loop(0, blocks // unroll, deposit, 0)
+
+    select = jnp.where(lax.broadcasted_iota(jnp.int32, (64, blocks), 0) == target_ref[...], 1.0, 0.0).astype(jnp.bfloat16)
+
+    def gather(pair, carry):
+        pieces = [split(block_sums[pl.ds(pl.multiple_of((2 * pair + k) * blocks, blocks), blocks), :]) for k in range(2)]
+        hi = jnp.concatenate([pieces[0][0], pieces[1][0]], 1)
+        lo = jnp.concatenate([pieces[0][1], pieces[1][1]], 1)
+        value = (jnp.dot(select, hi, preferred_element_type=jnp.float32)
+                 + jnp.dot(select, lo, preferred_element_type=jnp.float32))
+        for k in range(2):
+            for tr in range(4):
+                tiles[tr, pl.ds(pl.multiple_of((2 * pair + k) * 16, 16), 16), :] = value[tr * 16:tr * 16 + 16, k * 128:k * 128 + 128]
+        return carry
+
+    lax.fori_loop(0, TR, gather, 0)
     pl.semaphore_wait(barrier, bands - 1 + lons - 1)
 
     upward = pltpu.make_async_remote_copy(
-        src_ref=tiles_ref.at[pl.ds(0, 16)], dst_ref=halo.at[1], send_sem=halo_send.at[0], recv_sem=halo_recv.at[1],
+        src_ref=tiles.at[0], dst_ref=halo.at[1], send_sem=halo_send.at[0], recv_sem=halo_recv.at[1],
         device_id=(above, lon), device_id_type=MESH)
     downward = pltpu.make_async_remote_copy(
-        src_ref=tiles_ref.at[pl.ds(48, 16)], dst_ref=halo.at[0], send_sem=halo_send.at[1], recv_sem=halo_recv.at[0],
+        src_ref=tiles.at[3], dst_ref=halo.at[0], send_sem=halo_send.at[1], recv_sem=halo_recv.at[0],
         device_id=(below, lon), device_id_type=MESH)
     upward.start()
     downward.start()
@@ -116,8 +166,8 @@
             for tr in range(2):
                 place = v * 128 + h * 64 + tr * 32
                 for k in range(2):
-                    tile = 2 * (v + 4 * h) + k
-                    value = tiles_ref[16 * (tr + 1) + tile] + halo[tr, tile]
+                    rows = pl.ds(2 * (v + 4 * h) + k, 32, stride=16)
+                    value = tiles[tr + 1, rows, :] + halo[tr, rows, :]
                     hi, lo = split(value)
                     g_hi[pl.ds(place, 32), pl.ds(k * 128, 128)] = hi
                     g_lo[pl.ds(place, 32), pl.ds(k * 128, 128)] = lo
@@ -225,16 +275,19 @@
     pltpu.make_async_copy(total.at[others], total.at[others], a_send).wait()
 
 
-def spectra(tiles, orders, bands, lons, subs=4, lag=2):
+def spectra(targets, qu, off, rb, cb, orders, bands, lons, subs=4, lag=2, unroll=16):
     V = pl.BlockSpec(memory_space=pltpu.VMEM)
     f32, bf16 = jnp.float32, jnp.bfloat16
+    blocks = rb.shape[0]
     return pl.pallas_call(
-        functools.partial(spectra_kernel, bands, lons, subs, lag),
+        functools.partial(spectra_kernel, bands, lons, subs, lag, unroll),
         out_shape=jax.ShapeDtypeStruct((2, 4, bands * ROWS_DEV), f32),
-        in_specs=[V, V],
+        in_specs=[V] * 6,
         out_specs=V,
         scratch_shapes=[
-            pltpu.VMEM((2, 16, 32, 128), f32),
+            pltpu.VMEM((2 * TR * blocks, TC), f32),
+            pltpu.VMEM((4, 512, TC), f32),
+            pltpu.VMEM((2, 512, TC), f32),
             pltpu.VMEM((1024, 128), f32),
             pltpu.VMEM((subs, 2, 256, 256), bf16),
             pltpu.VMEM((subs, 2, 256, 256), bf16),
@@ -254,61 +307,14 @@
             pltpu.SemaphoreType.DMA,
         ],
         compiler_params=pltpu.CompilerParams(collective_id=0, has_side_effects=True, vmem_limit_bytes=40 * 1024 * 1024),
-    )(tiles, orders)
-
-
-def deposit_kernel(unroll, tile_ref, qu_ref, off_ref, rb_ref, cb_ref, tiles_ref):
-    tiles_ref[...] = jnp.zeros_like(tiles_ref)
-    pos = lax.broadcasted_iota(jnp.int32, (16, 128), 0)
-
-    def one(n):
-        row = pl.ds(n, 1)
-        cb = cb_ref[row, :]
-        col_o = (pos - cb) & 15
-        d = col_o.astype(jnp.float32) - (off_ref[1, row, :] + 3.0)
-        v = jnp.exp2(d * d * TAP_SCALE)
-        v_hi, v_lo = split(v)
-        group = jnp.where(col_o < 8, cb + col_o - pos, -16).astype(jnp.bfloat16)
-        zero = jnp.zeros((16, 128), jnp.bfloat16)
-        hi, lo = [], []
-        for ch in range(8):
-            m = group == jnp.bfloat16(16 * ch)
-            hi.append(jnp.where(m, v_hi, zero))
-            lo.append(jnp.where(m, v_lo, zero))
-        cols = jnp.concatenate([jnp.concatenate(hi, 0), jnp.concatenate(lo, 0)], 1)
-        row_o = (pos - rb_ref[row, :]) & 15
-        e = row_o.astype(jnp.float32) - (off_ref[0, row, :] + 3.0)
-        a = jnp.where(row_o < 8, jnp.exp2(e * e * TAP_SCALE), 0.0)
-        q_hi, q_lo = split(a * qu_ref[0, row, :])
-        u_hi, u_lo = split(a * qu_ref[1, row, :])
-        half = jnp.concatenate([q_hi, u_hi, q_lo, u_lo], 0)
-        rows = jnp.concatenate([half, half], 1)
-        out = lax.dot_general(rows, cols, (((1,), (1,)), ((), ())), preferred_element_type=jnp.float32)
-        return out[:32] + out[32:]
-
-    def step(i, carry):
-        outs = [(tile_ref[i * unroll + j], one(i * unroll + j)) for j in range(unroll)]
-        for t, o in outs:
-            tiles_ref[t] += o
-        return carry
-
-    lax.fori_loop(0, 256 // unroll, step, 0)
-
-def deposit(qu, off, rb, cb, tile, unroll=8):
-    V = pl.BlockSpec(memory_space=pltpu.VMEM)
-    return pl.pallas_call(
-        functools.partial(deposit_kernel, unroll),
-        out_shape=pltpu.VMEM((64, 32, 128), jnp.float32),
-        in_specs=[pl.BlockSpec(memory_space=pltpu.SMEM), V, V, V, V],
-        out_specs=V,
-    )(tile, qu, off, rb, cb)
+    )(targets, qu, off, rb, cb, orders)
 
 
 def body(qu_values, tap_offsets, row_base, col_base, tile_of_block, m_orders):
     bands = lax.axis_size("band")
     lons = lax.axis_size("lon")
-    tiles = deposit(qu_values, tap_offsets, row_base, col_base, tile_of_block, 32)
-    return spectra(tiles, m_orders.reshape(8, 128), bands, lons)
+    return spectra(tile_of_block.reshape(1, -1), qu_values, tap_offsets, row_base, col_base, m_orders.reshape(8, 128),
+                   bands, lons)
 
 
 def solution(mesh):

time: 50.5 us -> 54.6 us (1.081)
  local copies, waits for them, and re-layouts: 0.66 us -> 5.73 us
  Pallas kernels: 49.7 us -> 48.6 us
    unnamed x3 -> x13, local copies, waits for them, and re-layouts: 0.66 us -> 5.73 us
    pallas_call x2 -> x1, Pallas kernels: 49.7 us -> 48.6 us  [spectra(): pl.pallas_call(functools.partial(spectra_kernel, bands, lons, subs, lag,...]
where the time goes in v3:
time: 54.6 us; the launch traced here: 54.4 us
  Pallas kernels  48.6 us (89%)
  local copies, waits for them, and re-layouts  5.73 us (10%)
    pallas_call x1, Pallas kernels, spectra(): pl.pallas_call(functools.partial(spectra_kernel, bands, lons, subs, lag,...  48.6 us
    unnamed x13, local copies, waits for them, and re-layouts  5.73 us

profile of v3, /device:TPU:1, one launch (start us, length us, event | category | flops | bytes accessed | tf_op | source)
XLA Modules:
  0.0 54.4 jit_solution(8887202340065560782)
XLA Ops:
  0.0 0.0 copy-start.5
  0.0 0.7 %copy-done.5 = s32[256]{0:T(256)S(1)} copy-done((s32[256]{0:T(256)S(1)}, s32[256]{0:T(256)}, u32[]{:S(2)}) %copy-start.5) | copy-done | bytes 1048
  0.7 0.0 copy-start
  0.7 0.9 %copy-done = f32[2,256,128]{2,1,0:T(8,128)S(1)} copy-done((f32[2,256,128]{2,1,0:T(8,128)S(1)}, f32[2,256,128]{2,1,0:T(8,128)}, u32[]{:S(2)}) %copy-start) | copy-done | bytes 262168
  1.6 0.0 copy-start.1
  1.6 0.9 %copy-done.1 = f32[2,256,128]{2,1,0:T(8,128)S(1)} copy-done((f32[2,256,128]{2,1,0:T(8,128)S(1)}, f32[2,256,128]{2,1,0:T(8,128)}, u32[]{:S(2)}) %copy-start.1) | copy-done | bytes 262168
  2.6 0.0 copy-start.2
  2.6 0.9 %copy-done.2 = s32[256,128]{1,0:T(8,128)S(1)} copy-done((s32[256,128]{1,0:T(8,128)S(1)}, s32[256,128]{1,0:T(8,128)}, u32[]{:S(2)}) %copy-start.2) | copy-done | bytes 131096
  3.5 0.0 copy-start.3
  3.5 0.9 %copy-done.3 = s32[256,128]{1,0:T(8,128)S(1)} copy-done((s32[256,128]{1,0:T(8,128)S(1)}, s32[256,128]{1,0:T(8,128)}, u32[]{:S(2)}) %copy-start.3) | copy-done | bytes 131096
  4.4 0.0 copy-start.4
  4.4 0.7 %copy-done.4 = s32[1024]{0:T(1024)S(1)} copy-done((s32[1024]{0:T(1024)S(1)}, s32[1024]{0:T(1024)}, u32[]{:S(2)}) %copy-start.4) | copy-done | bytes 4120
  5.1 48.6 %shard_map.64 = f32[2,4,4096]{2,1,0:T(4,128)S(1)} custom-call(s32[1,256]{1,0:T(1,128)S(1)} %bitcast.3, f32[2,256,128]{2,1,0:T(8,128)S(1)} %copy-done, f32[2,256,128]{2,1,0:T(8,128)S(1)} %copy-done.1, s32[256,128]{1,0:T(8,128)S(1)} %copy-done.2, s32[256,128]{1,0:T(8,128)S(1)} %copy-done.3, s32[8,128]{1,0:T(8,128)S(1)} %bitcast.2), custom_call_target="tpu_custom_call" | custom-call | tf_op jit(solution)/shard_map/pallas_call | solution.py:282
  53.7 0.7 %copy.8 = f32[2,4,4096]{2,1,0:T(4,128)} copy(f32[2,4,4096]{2,1,0:T(4,128)S(1)} %shard_map.64) | data formatting | bytes 262144
Async XLA Ops:
  0.0 0.7 %copy-start.5 = (s32[256]{0:T(256)S(1)}, s32[256]{0:T(256)}, u32[]{:S(2)}) copy-start(s32[256]{0:T(256)} %param.10) | copy-start | bytes 3076
  0.7 0.9 %copy-start = (f32[2,256,128]{2,1,0:T(8,128)S(1)}, f32[2,256,128]{2,1,0:T(8,128)}, u32[]{:S(2)}) copy-start(f32[2,256,128]{2,1,0:T(8,128)} %qu_ref.1) | copy-start | bytes 786436
  1.6 0.9 %copy-start.1 = (f32[2,256,128]{2,1,0:T(8,128)S(1)}, f32[2,256,128]{2,1,0:T(8,128)}, u32[]{:S(2)}) copy-start(f32[2,256,128]{2,1,0:T(8,128)} %off_ref.1) | copy-start | bytes 786436
  2.6 0.9 %copy-start.2 = (s32[256,128]{1,0:T(8,128)S(1)}, s32[256,128]{1,0:T(8,128)}, u32[]{:S(2)}) copy-start(s32[256,128]{1,0:T(8,128)} %rb_ref.1) | copy-start | bytes 393220
  3.5 0.9 %copy-start.3 = (s32[256,128]{1,0:T(8,128)S(1)}, s32[256,128]{1,0:T(8,128)}, u32[]{:S(2)}) copy-start(s32[256,128]{1,0:T(8,128)} %cb_ref.1) | copy-start | bytes 393220
  4.4 0.7 %copy-start.4 = (s32[1024]{0:T(1024)S(1)}, s32[1024]{0:T(1024)}, u32[]{:S(2)}) copy-start(s32[1024]{0:T(1024)} %param.11) | copy-start | bytes 12292

commit v4 on v3

--- a/solution.py
+++ b/solution.py
@@ -36,9 +36,9 @@
     return lax.dot_general(a, b, (((1,), (1,)), ((), ())), preferred_element_type=jnp.float32)
 
 
-def spectra_kernel(bands, lons, subs, lag, unroll, target_ref, qu_ref, off_ref, rb_ref, cb_ref, orders_ref, out_ref,
-                   block_sums, tiles, halo, order_col, t_hi, t_lo, turn, spin, g_hi, g_lo, part, arrived, total, landed,
-                   halo_send, halo_recv, x_send, x_recv, a_send, a_recv):
+def spectra_kernel(bands, lons, subs, lag, unroll, target_hbm, qu_hbm, off_hbm, rb_hbm, cb_hbm, orders_hbm, out_ref,
+                   target_ref, qu_ref, off_ref, rb_ref, cb_ref, orders_ref, keys_row, keys, sums, tiles, halo, order_col, t_hi, t_lo,
+                   turn, spin, g_hi, g_lo, part, arrived, total, landed, in_sem, keys_sem, halo_send, halo_recv, x_send, x_recv, a_send, a_recv):
     band = lax.axis_index("band")
     lon = lax.axis_index("lon")
     run = bands // subs
@@ -50,9 +50,45 @@
     below = lax.rem(band + 1, bands)
     blocks = rb_ref.shape[0]
 
+    arrays = ((target_hbm, target_ref), (cb_hbm, cb_ref), (rb_hbm, rb_ref), (off_hbm, off_ref), (qu_hbm, qu_ref),
+              (orders_hbm, orders_ref))
+    inputs = [pltpu.make_async_copy(source, here, in_sem.at[i]) for i, (source, here) in enumerate(arrays)]
+    for copy in inputs:
+        copy.start()
+
     barrier = pltpu.get_barrier_semaphore()
     for step in range(1, lons):
         pl.semaphore_signal(barrier, inc=1, device_id=(band, lax.rem(lon + step, lons)), device_id_type=MESH)
+
+    inputs[0].wait()
+    lane128 = lax.broadcasted_iota(jnp.int32, (1, 128), 1)
+    row_keys, col_keys = [], []
+    for h in range(blocks // 128):
+        row = (target_ref[:, h * 128:h * 128 + 128] * blocks + (lane128 + h * 128)).astype(jnp.float32)
+        row_keys.append(row)
+        col_keys.append(jnp.transpose(jnp.broadcast_to(row, (128, 128))))
+    ranks = []
+    for col in col_keys:
+        before = jnp.zeros((128, 128), jnp.float32)
+        for row in row_keys:
+            before = before + jnp.where(row < col, 1.0, 0.0)
+        ranks.append(jnp.sum(before, 1, keepdims=True))
+    upto = jnp.zeros((1, 128), jnp.float32)
+    for col in col_keys:
+        limit = ((lane128 + 1) * blocks).astype(jnp.float32)
+        upto = upto + jnp.sum(jnp.where(col < limit, 1.0, 0.0), 0, keepdims=True)
+    for h in range(blocks // 128):
+        place = (lane128 + h * 128).astype(jnp.float32)
+        row = jnp.zeros((1, 128), jnp.float32)
+        for col, rank in zip(col_keys, ranks):
+            row = row + jnp.sum(jnp.where(rank == place, col, 0.0), 0, keepdims=True)
+        keys_row[pl.ds(h, 1), :] = row.astype(jnp.int32)
+    keys_row[pl.ds(blocks // 128, 1), :] = upto.astype(jnp.int32)
+    to_scalars = pltpu.make_async_copy(keys_row, keys, keys_sem)
+    to_scalars.start()
+    to_scalars.wait()
+    for copy in inputs[1:]:
+        copy.wait()
 
     pos = lax.broadcasted_iota(jnp.int32, (TR, 128), 0)
 
@@ -80,6 +116,7 @@
         return out[:2 * TR] + out[2 * TR:]
 
     greets = bands * unroll // blocks
+    key_bits = blocks.bit_length() - 1
 
     def deposit(i, carry):
         for j in range(greets):
@@ -89,34 +126,33 @@
             def _():
                 pl.semaphore_signal(barrier, inc=1, device_id=(lax.rem(band + step, bands), lon), device_id_type=MESH)
 
+        running, last_tile = carry
         for j in range(unroll):
-            n = i * unroll + j
-            block_sums[pl.ds(n, 2 * TR, stride=blocks), :] = block_tile(n)
+            place = i * unroll + j
+            key = keys[place // 128, place % 128]
+            tile = key >> key_bits
+            same = jnp.where(tile == last_tile, 1.0, 0.0)
+            running = running * same + block_tile(key & (blocks - 1))
+            sums[place] = running
+            last_tile = tile
+        return running, last_tile
+
+    lax.fori_loop(0, blocks // unroll, deposit, (jnp.zeros((2 * TR, TC), jnp.float32), jnp.int32(-1)))
+
+    def gather(tile, carry):
+        last = (keys[blocks // 128, tile] - 1) & (blocks - 1)
+        found = jnp.where((keys[last >> 7, last & 127] >> key_bits) == tile, 1.0, 0.0)
+        tiles[tile] = sums[last] * found
         return carry
 
-    lax.fori_loop(0, blocks // unroll, deposit, 0)
-
-    select = jnp.where(lax.broadcasted_iota(jnp.int32, (64, blocks), 0) == target_ref[...], 1.0, 0.0).astype(jnp.bfloat16)
-
-    def gather(pair, carry):
-        pieces = [split(block_sums[pl.ds(pl.multiple_of((2 * pair + k) * blocks, blocks), blocks), :]) for k in range(2)]
-        hi = jnp.concatenate([pieces[0][0], pieces[1][0]], 1)
-        lo = jnp.concatenate([pieces[0][1], pieces[1][1]], 1)
-        value = (jnp.dot(select, hi, preferred_element_type=jnp.float32)
-                 + jnp.dot(select, lo, preferred_element_type=jnp.float32))
-        for k in range(2):
-            for tr in range(4):
-                tiles[tr, pl.ds(pl.multiple_of((2 * pair + k) * 16, 16), 16), :] = value[tr * 16:tr * 16 + 16, k * 128:k * 128 + 128]
-        return carry
-
-    lax.fori_loop(0, TR, gather, 0)
+    lax.fori_loop(0, 64, gather, 0, unroll=8)
     pl.semaphore_wait(barrier, bands - 1 + lons - 1)
 
     upward = pltpu.make_async_remote_copy(
-        src_ref=tiles.at[0], dst_ref=halo.at[1], send_sem=halo_send.at[0], recv_sem=halo_recv.at[1],
+        src_ref=tiles.at[pl.ds(0, 16)], dst_ref=halo.at[1], send_sem=halo_send.at[0], recv_sem=halo_recv.at[1],
         device_id=(above, lon), device_id_type=MESH)
     downward = pltpu.make_async_remote_copy(
-        src_ref=tiles.at[3], dst_ref=halo.at[0], send_sem=halo_send.at[1], recv_sem=halo_recv.at[0],
+        src_ref=tiles.at[pl.ds(48, 16)], dst_ref=halo.at[0], send_sem=halo_send.at[1], recv_sem=halo_recv.at[0],
         device_id=(below, lon), device_id_type=MESH)
     upward.start()
     downward.start()
@@ -138,15 +174,16 @@
         first = group * per_group + 2 * ell
         m = jnp.concatenate([order_col[pl.ds(first + place, run, stride=2 * lons), :] for place in range(2)], 0)
         rows = pl.ds(pl.multiple_of(ell * 2 * run, 2 * run), 2 * run)
+        sine_rows = pl.ds(pl.multiple_of(per_group + ell * 2 * run, 2 * run), 2 * run)
         for side in range(2):
             c, s = cos_sin(m * (low_columns + side * (128.0 / 2048)))
             c_hi, c_lo = split(c)
             s_hi, s_lo = split(-s)
             cols = pl.ds(side * 128, 128)
-            t_hi[group, 0, rows, cols] = c_hi
-            t_lo[group, 0, rows, cols] = c_lo
-            t_hi[group, 1, rows, cols] = s_hi
-            t_lo[group, 1, rows, cols] = s_lo
+            t_hi[group, rows, cols] = c_hi
+            t_lo[group, rows, cols] = c_lo
+            t_hi[group, sine_rows, cols] = s_hi
+            t_lo[group, sine_rows, cols] = s_lo
         c, s = cos_sin(m * (256.0 / 2048))
         turn[group, 0, rows, :] = c
         turn[group, 1, rows, :] = -s
@@ -162,43 +199,45 @@
     downward.wait_recv()
 
     for v in range(4):
-        for h in range(2):
-            for tr in range(2):
-                place = v * 128 + h * 64 + tr * 32
-                for k in range(2):
-                    rows = pl.ds(2 * (v + 4 * h) + k, 32, stride=16)
-                    value = tiles[tr + 1, rows, :] + halo[tr, rows, :]
-                    hi, lo = split(value)
-                    g_hi[pl.ds(place, 32), pl.ds(k * 128, 128)] = hi
-                    g_lo[pl.ds(place, 32), pl.ds(k * 128, 128)] = lo
+        for k in range(2):
+            pieces = []
+            for h in range(2):
+                for tr in range(2):
+                    tile = 2 * (v + 4 * h) + k
+                    pieces.append(tiles[16 * (tr + 1) + tile] + halo[tr, tile])
+            hi, lo = split(jnp.transpose(jnp.concatenate(pieces, 0)))
+            g_hi[pl.ds(k * 128, 128), pl.ds(v * 128, 128)] = hi
+            g_lo[pl.ds(k * 128, 128), pl.ds(v * 128, 128)] = lo
 
     is_real = lane < 64
 
     def transform(group):
-        for side in range(2):
-            rows = pl.ds(side * 128, 128)
-            cs = []
-            for q in range(2):
-                hi = t_hi[group, q, rows, :]
-                lo = t_lo[group, q, rows, :]
-                cs.append(nt_dot(hi, g_hi[...]) + nt_dot(hi, g_lo[...]) + nt_dot(lo, g_hi[...]))
-            c, s = cs
-            wr = turn[group, 0, rows, :]
-            wi = turn[group, 1, rows, :]
-            re, im = c[:, 384:], s[:, 384:]
-            for v in (2, 1, 0):
-                re, im = (re * wr - im * wi + c[:, v * 128:v * 128 + 128],
-                          re * wi + im * wr + s[:, v * 128:v * 128 + 128])
-            pr = spin[group, 0, rows, :]
-            pi = spin[group, 1, rows, :]
-            zr = re * pr - im * pi
-            zi = re * pi + im * pr
-            zr = zr + pltpu.roll(zr, 64, 1)
-            zi = zi + pltpu.roll(zi, 64, 1)
-            z = jnp.where(is_real, zr, zi)
-            for k in range(128 // run):
-                ell, place = divmod(side * (128 // run) + k, 2)
-                part[group, ell, pl.ds(place, run, stride=2), :] = z[k * run:(k + 1) * run]
+        def product(v):
+            cols = pl.ds(v * 128, 256)
+            value = (jnp.dot(t_hi[group], g_hi[:, cols], preferred_element_type=jnp.float32)
+                     + jnp.dot(t_hi[group], g_lo[:, cols], preferred_element_type=jnp.float32)
+                     + jnp.dot(t_lo[group], g_hi[:, cols], preferred_element_type=jnp.float32))
+            return value[:per_group], value[per_group:]
+
+        wr = turn[group, 0]
+        wi = turn[group, 1]
+        re = im = None
+        for v in (2, 0):
+            c, s = product(v)
+            for side in (1, 0):
+                c1 = c[:, side * 128:side * 128 + 128]
+                s1 = s[:, side * 128:side * 128 + 128]
+                re, im = (c1, s1) if re is None else (re * wr - im * wi + c1, re * wi + im * wr + s1)
+        pr = spin[group, 0]
+        pi = spin[group, 1]
+        zr = re * pr - im * pi
+        zi = re * pi + im * pr
+        zr = zr + pltpu.roll(zr, 64, 1)
+        zi = zi + pltpu.roll(zi, 64, 1)
+        z = jnp.where(is_real, zr, zi)
+        for k in range(per_group // run):
+            ell, place = divmod(k, 2)
+            part[group, ell, pl.ds(place, run, stride=2), :] = z[k * run:(k + 1) * run]
 
     def over_lon(step, group, sub):
         ell = lax.rem(lon + step, lons)
@@ -275,30 +314,40 @@
     pltpu.make_async_copy(total.at[others], total.at[others], a_send).wait()
 
 
-def spectra(targets, qu, off, rb, cb, orders, bands, lons, subs=4, lag=2, unroll=16):
+def spectra(targets, qu, off, rb, cb, orders, bands, lons, subs=4, lag=2, unroll=32):
     V = pl.BlockSpec(memory_space=pltpu.VMEM)
     f32, bf16 = jnp.float32, jnp.bfloat16
     blocks = rb.shape[0]
     return pl.pallas_call(
         functools.partial(spectra_kernel, bands, lons, subs, lag, unroll),
         out_shape=jax.ShapeDtypeStruct((2, 4, bands * ROWS_DEV), f32),
-        in_specs=[V] * 6,
+        in_specs=[pl.BlockSpec(memory_space=pl.ANY)] * 6,
         out_specs=V,
         scratch_shapes=[
-            pltpu.VMEM((2 * TR * blocks, TC), f32),
-            pltpu.VMEM((4, 512, TC), f32),
-            pltpu.VMEM((2, 512, TC), f32),
+            pltpu.VMEM(targets.shape, jnp.int32),
+            pltpu.VMEM(qu.shape, f32),
+            pltpu.VMEM(off.shape, f32),
+            pltpu.VMEM(rb.shape, jnp.int32),
+            pltpu.VMEM(cb.shape, jnp.int32),
+            pltpu.VMEM(orders.shape, jnp.int32),
+            pltpu.VMEM((8, 128), jnp.int32),
+            pltpu.SMEM((8, 128), jnp.int32),
+            pltpu.VMEM((blocks, 2 * TR, TC), f32),
+            pltpu.VMEM((64, 2 * TR, TC), f32),
+            pltpu.VMEM((2, 16, 2 * TR, TC), f32),
             pltpu.VMEM((1024, 128), f32),
-            pltpu.VMEM((subs, 2, 256, 256), bf16),
-            pltpu.VMEM((subs, 2, 256, 256), bf16),
+            pltpu.VMEM((subs, 512, 256), bf16),
+            pltpu.VMEM((subs, 512, 256), bf16),
             pltpu.VMEM((subs, 2, 256, 128), f32),
             pltpu.VMEM((subs, 2, 256, 128), f32),
-            pltpu.VMEM((512, 256), bf16),
-            pltpu.VMEM((512, 256), bf16),
+            pltpu.VMEM((256, 512), bf16),
+            pltpu.VMEM((256, 512), bf16),
             pltpu.VMEM((subs, lons, 256 // subs, 128), f32),
             pltpu.VMEM((subs, lons, 256 // subs, 128), f32),
             pltpu.VMEM((256, 128), f32),
             pltpu.VMEM((256, 128), f32),
+            pltpu.SemaphoreType.DMA((6,)),
+            pltpu.SemaphoreType.DMA,
             pltpu.SemaphoreType.DMA((2,)),
             pltpu.SemaphoreType.DMA((2,)),
             pltpu.SemaphoreType.DMA((lons, subs)),
@@ -306,7 +355,7 @@
             pltpu.SemaphoreType.DMA,
             pltpu.SemaphoreType.DMA,
         ],
-        compiler_params=pltpu.CompilerParams(collective_id=0, has_side_effects=True, vmem_limit_bytes=40 * 1024 * 1024),
+        compiler_params=pltpu.CompilerParams(collective_id=0, has_side_effects=True, vmem_limit_bytes=63 * 1024 * 1024),
     )(targets, qu, off, rb, cb, orders)
 
 

time: 54.6 us -> 49 us (0.90)
  local copies, waits for them, and re-layouts: 5.73 us -> 1.57 us
  Pallas kernels: 48.6 us -> 47.3 us
    unnamed x13 -> x1, local copies, waits for them, and re-layouts: 5.73 us -> 1.57 us
    pallas_call x1, Pallas kernels: 48.6 us -> 47.3 us  [spectra(): pl.pallas_call(functools.partial(spectra_kernel, bands, lons, subs, lag,...]
where the time goes in v4:
time: 49 us; the launch traced here: 48.8 us
  Pallas kernels  47.3 us (97%)
  local copies, waits for them, and re-layouts  1.57 us (3%)
    pallas_call x1, Pallas kernels, spectra(): pl.pallas_call(functools.partial(spectra_kernel, bands, lons, subs, lag,...  47.3 us
    unnamed x1, local copies, waits for them, and re-layouts  1.57 us

profile of v4, /device:TPU:1, one launch (start us, length us, event | category | flops | bytes accessed | tf_op | source)
XLA Modules:
  0.0 48.8 jit_solution(8704418267492497814)
XLA Ops:
  0.0 47.3 %shard_map.64 = f32[2,4,4096]{2,1,0:T(4,128)} custom-call(s32[1,256]{1,0:T(1,128)} %bitcast.3, f32[2,256,128]{2,1,0:T(8,128)} %qu_hbm.1, f32[2,256,128]{2,1,0:T(8,128)} %off_hbm.1, s32[256,128]{1,0:T(8,128)} %rb_hbm.1, s32[256,128]{1,0:T(8,128)} %cb_hbm.1, s32[8,128]{1,0:T(8,128)} %bitcast.2), custom_call_target="tpu_custom_call" | custom-call | tf_op jit(solution)/shard_map/pallas_call | solution.py:321
  47.3 1.6 %copy.8 = f32[2,4,4096]{2,1,0:T(4,128)} copy(f32[2,4,4096]{2,1,0:T(4,128)} %shard_map.64) | data formatting | bytes 262144

commit v5 on v4

--- a/solution.py
+++ b/solution.py
@@ -38,7 +38,7 @@
 
 def spectra_kernel(bands, lons, subs, lag, unroll, target_hbm, qu_hbm, off_hbm, rb_hbm, cb_hbm, orders_hbm, out_ref,
                    target_ref, qu_ref, off_ref, rb_ref, cb_ref, orders_ref, keys_row, keys, sums, tiles, halo, order_col, t_hi, t_lo,
-                   turn, spin, g_hi, g_lo, part, arrived, total, landed, in_sem, keys_sem, halo_send, halo_recv, x_send, x_recv, a_send, a_recv):
+                   turn, spin, g_hi, g_lo, part, arrived, total, landed, ready, in_sem, keys_sem, halo_send, halo_recv, x_send, x_recv, a_send, a_recv):
     band = lax.axis_index("band")
     lon = lax.axis_index("lon")
     run = bands // subs
@@ -56,9 +56,19 @@
     for copy in inputs:
         copy.start()
 
+    width = bands // 8
+    first_of_row = band // width * width
+
+    def in_row(step):
+        return first_of_row + lax.rem(band + step, width)
+
     barrier = pltpu.get_barrier_semaphore()
-    for step in range(1, lons):
-        pl.semaphore_signal(barrier, inc=1, device_id=(band, lax.rem(lon + step, lons)), device_id_type=MESH)
+    greeted = [(above, lon), (below, lon)]
+    greeted += [(band, lax.rem(lon + step, lons)) for step in range(1, lons)]
+    greeted += [(in_row(step), lon) for step in range(1, width)]
+    greeted += [(lax.rem(band + step * width, bands), lon) for step in range(1, bands // width)]
+    for place in greeted:
+        pl.semaphore_signal(barrier, inc=1, device_id=place, device_id_type=MESH)
 
     inputs[0].wait()
     lane128 = lax.broadcasted_iota(jnp.int32, (1, 128), 1)
@@ -115,17 +125,9 @@
         out = nt_dot(jnp.concatenate([half, half], 1), cols)
         return out[:2 * TR] + out[2 * TR:]
 
-    greets = bands * unroll // blocks
     key_bits = blocks.bit_length() - 1
 
     def deposit(i, carry):
-        for j in range(greets):
-            step = i * greets + j
-
-            @pl.when(step > 0)
-            def _():
-                pl.semaphore_signal(barrier, inc=1, device_id=(lax.rem(band + step, bands), lon), device_id_type=MESH)
-
         running, last_tile = carry
         for j in range(unroll):
             place = i * unroll + j
@@ -146,7 +148,7 @@
         return carry
 
     lax.fori_loop(0, 64, gather, 0, unroll=8)
-    pl.semaphore_wait(barrier, bands - 1 + lons - 1)
+    pl.semaphore_wait(barrier, len(greeted))
 
     upward = pltpu.make_async_remote_copy(
         src_ref=tiles.at[pl.ds(0, 16)], dst_ref=halo.at[1], send_sem=halo_send.at[0], recv_sem=halo_recv.at[1],
@@ -156,6 +158,8 @@
         device_id=(below, lon), device_id_type=MESH)
     upward.start()
     downward.start()
+    for step in range(1, width):
+        pl.semaphore_signal(ready, inc=1, device_id=(in_row(step), lon), device_id_type=MESH)
 
     lane = lax.broadcasted_iota(jnp.int32, (1, 128), 1)
     half = lane // 64
@@ -246,15 +250,24 @@
             send_sem=x_send.at[step, sub], recv_sem=x_recv.at[lons - step, sub],
             device_id=(band, ell), device_id_type=MESH)
 
+    def far(step):
+        return -min(step // 2 % 8, 8 - step // 2 % 8)
+
+    def group_of(sub):
+        ahead = jnp.int32(0)
+        for i, step in enumerate(sorted(range(1, subs), key=lambda step: -min(step, subs - step))):
+            ahead = jnp.where(sub == i, step, ahead)
+        return lax.rem(quarter + ahead, subs)
+
     def send_part(sub, carry):
-        group = lax.rem(quarter + sub, subs)
+        group = group_of(sub)
         transform(group)
         for step in (2, 1, 3):
             over_lon(step, group, sub).start()
         return carry
 
     def send_total(sub, carry):
-        group = lax.rem(quarter + sub, subs)
+        group = group_of(sub)
         value = part[group, lon]
         for step in range(1, lons):
             over_lon(step, group, sub).wait_recv()
@@ -262,22 +275,27 @@
         rows = pl.ds(pl.multiple_of(group * per_sub, per_sub), per_sub)
         total[rows, :] = value
 
-        def send_one(step, carry):
-            target = group * run + lax.rem(band + step, run)
-
-            @pl.when(target != band)
-            def _():
-                pltpu.make_async_remote_copy(
-                    src_ref=total.at[pl.ds(2 * target, 2), :], dst_ref=landed.at[pl.ds(2 * band, 2), :],
-                    send_sem=a_send, recv_sem=a_recv, device_id=(target, lon), device_id_type=MESH).start()
-            return carry
-
-        return lax.fori_loop(0, run, send_one, carry)
+        def send_one(target):
+            pltpu.make_async_remote_copy(
+                src_ref=total.at[pl.ds(2 * target, 2), :], dst_ref=landed.at[pl.ds(2 * band, 2), :],
+                send_sem=a_send, recv_sem=a_recv, device_id=(target, lon), device_id_type=MESH).start()
+
+        for step in sorted(range(1, run), key=far):
+            send_one(group * run + lax.rem(band + step, run))
+
+        @pl.when(group != quarter)
+        def _():
+            send_one(group * run + lax.rem(band, run))
+        return carry
 
     def pipeline(sub, carry):
         @pl.when(sub < subs)
         def _():
             send_part(sub, 0)
+
+        @pl.when(sub == lag)
+        def _():
+            pl.semaphore_wait(ready, width - 1)
 
         @pl.when(sub >= lag)
         def _():
@@ -309,12 +327,12 @@
     downward.wait_send()
     for sub in range(subs):
         for step in range(1, lons):
-            over_lon(step, lax.rem(quarter + sub, subs), sub).wait_send()
+            over_lon(step, group_of(sub), sub).wait_send()
     others = pl.ds(0, per_lon - 2)
     pltpu.make_async_copy(total.at[others], total.at[others], a_send).wait()
 
 
-def spectra(targets, qu, off, rb, cb, orders, bands, lons, subs=4, lag=2, unroll=32):
+def spectra(targets, qu, off, rb, cb, orders, bands, lons, subs=4, lag=3, unroll=32):
     V = pl.BlockSpec(memory_space=pltpu.VMEM)
     f32, bf16 = jnp.float32, jnp.bfloat16
     blocks = rb.shape[0]
@@ -346,6 +364,7 @@
             pltpu.VMEM((subs, lons, 256 // subs, 128), f32),
             pltpu.VMEM((256, 128), f32),
             pltpu.VMEM((256, 128), f32),
+            pltpu.SemaphoreType.REGULAR,
             pltpu.SemaphoreType.DMA((6,)),
             pltpu.SemaphoreType.DMA,
             pltpu.SemaphoreType.DMA((2,)),

time: 49 us -> 41.3 us (0.84)
  Pallas kernels: 47.3 us -> 39.6 us
    pallas_call x1, Pallas kernels: 47.3 us -> 39.6 us  [spectra(): pl.pallas_call(functools.partial(spectra_kernel, bands, lons, subs, lag,...]
where the time goes in v5:
time: 41.3 us; the launch traced here: 41.2 us
  Pallas kernels  39.6 us (96%)
  local copies, waits for them, and re-layouts  1.57 us (4%)
    pallas_call x1, Pallas kernels, spectra(): pl.pallas_call(functools.partial(spectra_kernel, bands, lons, subs, lag,...  39.6 us
    unnamed x1, local copies, waits for them, and re-layouts  1.57 us

profile of v5, /device:TPU:1, one launch (start us, length us, event | category | flops | bytes accessed | tf_op | source)
XLA Modules:
  0.0 41.2 jit_solution(12015689311121961678)
XLA Ops:
  0.0 39.6 %shard_map.64 = f32[2,4,4096]{2,1,0:T(4,128)} custom-call(s32[1,256]{1,0:T(1,128)} %bitcast.3, f32[2,256,128]{2,1,0:T(8,128)} %qu_hbm.1, f32[2,256,128]{2,1,0:T(8,128)} %off_hbm.1, s32[256,128]{1,0:T(8,128)} %rb_hbm.1, s32[256,128]{1,0:T(8,128)} %cb_hbm.1, s32[8,128]{1,0:T(8,128)} %bitcast.2), custom_call_target="tpu_custom_call" | custom-call | tf_op jit(solution)/shard_map/pallas_call | solution.py:339
  39.6 1.6 %copy.8 = f32[2,4,4096]{2,1,0:T(4,128)} copy(f32[2,4,4096]{2,1,0:T(4,128)} %shard_map.64) | data formatting | bytes 262144

commit v6 on v5

--- a/solution.py
+++ b/solution.py
@@ -83,17 +83,21 @@
         for row in row_keys:
             before = before + jnp.where(row < col, 1.0, 0.0)
         ranks.append(jnp.sum(before, 1, keepdims=True))
-    upto = jnp.zeros((1, 128), jnp.float32)
+    through = jnp.zeros((1, 128), jnp.float32)
+    ahead = jnp.zeros((1, 128), jnp.float32)
+    first_key = (lane128 * blocks).astype(jnp.float32)
     for col in col_keys:
-        limit = ((lane128 + 1) * blocks).astype(jnp.float32)
-        upto = upto + jnp.sum(jnp.where(col < limit, 1.0, 0.0), 0, keepdims=True)
+        ahead = ahead + jnp.sum(jnp.where(col < first_key, 1.0, 0.0), 0, keepdims=True)
+        through = through + jnp.sum(jnp.where(col < first_key + blocks, 1.0, 0.0), 0, keepdims=True)
+    last_place = jnp.where(through > ahead, through - 1.0, float(blocks))
     for h in range(blocks // 128):
         place = (lane128 + h * 128).astype(jnp.float32)
         row = jnp.zeros((1, 128), jnp.float32)
         for col, rank in zip(col_keys, ranks):
             row = row + jnp.sum(jnp.where(rank == place, col, 0.0), 0, keepdims=True)
         keys_row[pl.ds(h, 1), :] = row.astype(jnp.int32)
-    keys_row[pl.ds(blocks // 128, 1), :] = upto.astype(jnp.int32)
+    keys_row[pl.ds(blocks // 128, 1), :] = last_place.astype(jnp.int32)
+    sums[blocks] = jnp.zeros((2 * TR, TC), jnp.float32)
     to_scalars = pltpu.make_async_copy(keys_row, keys, keys_sem)
     to_scalars.start()
     to_scalars.wait()
@@ -122,7 +126,7 @@
         q_hi, q_lo = split(a * qu_ref[0, row, :])
         u_hi, u_lo = split(a * qu_ref[1, row, :])
         half = jnp.concatenate([q_hi, u_hi, q_lo, u_lo], 0)
-        out = nt_dot(jnp.concatenate([half, half], 1), cols)
+        out = jnp.transpose(nt_dot(cols, jnp.concatenate([half, half], 1)))
         return out[:2 * TR] + out[2 * TR:]
 
     key_bits = blocks.bit_length() - 1
@@ -142,12 +146,11 @@
     lax.fori_loop(0, blocks // unroll, deposit, (jnp.zeros((2 * TR, TC), jnp.float32), jnp.int32(-1)))
 
     def gather(tile, carry):
-        last = (keys[blocks // 128, tile] - 1) & (blocks - 1)
-        found = jnp.where((keys[last >> 7, last & 127] >> key_bits) == tile, 1.0, 0.0)
-        tiles[tile] = sums[last] * found
+        tiles[tile] = sums[jnp.clip(keys[blocks // 128, tile], 0, blocks)]
         return carry
 
-    lax.fori_loop(0, 64, gather, 0, unroll=8)
+    lax.fori_loop(0, 16, gather, 0, unroll=16)
+    lax.fori_loop(48, 64, gather, 0, unroll=16)
     pl.semaphore_wait(barrier, len(greeted))
 
     upward = pltpu.make_async_remote_copy(
@@ -160,6 +163,8 @@
     downward.start()
     for step in range(1, width):
         pl.semaphore_signal(ready, inc=1, device_id=(in_row(step), lon), device_id_type=MESH)
+
+    lax.fori_loop(16, 48, gather, 0, unroll=16)
 
     lane = lax.broadcasted_iota(jnp.int32, (1, 128), 1)
     half = lane // 64
@@ -332,7 +337,7 @@
     pltpu.make_async_copy(total.at[others], total.at[others], a_send).wait()
 
 
-def spectra(targets, qu, off, rb, cb, orders, bands, lons, subs=4, lag=3, unroll=32):
+def spectra(targets, qu, off, rb, cb, orders, bands, lons, subs=4, lag=3, unroll=64):
     V = pl.BlockSpec(memory_space=pltpu.VMEM)
     f32, bf16 = jnp.float32, jnp.bfloat16
     blocks = rb.shape[0]
@@ -350,7 +355,7 @@
             pltpu.VMEM(orders.shape, jnp.int32),
             pltpu.VMEM((8, 128), jnp.int32),
             pltpu.SMEM((8, 128), jnp.int32),
-            pltpu.VMEM((blocks, 2 * TR, TC), f32),
+            pltpu.VMEM((blocks + 1, 2 * TR, TC), f32),
             pltpu.VMEM((64, 2 * TR, TC), f32),
             pltpu.VMEM((2, 16, 2 * TR, TC), f32),
             pltpu.VMEM((1024, 128), f32),

time: 41.3 us -> 39.5 us (0.956)
  Pallas kernels: 39.6 us -> 37.8 us
    pallas_call x1, Pallas kernels: 39.6 us -> 37.8 us  [spectra(): pl.pallas_call(functools.partial(spectra_kernel, bands, lons, subs, lag,...]
where the time goes in v6:
time: 39.5 us; the launch traced here: 39.4 us
  Pallas kernels  37.8 us (96%)
  local copies, waits for them, and re-layouts  1.57 us (4%)
    pallas_call x1, Pallas kernels, spectra(): pl.pallas_call(functools.partial(spectra_kernel, bands, lons, subs, lag,...  37.8 us
    unnamed x1, local copies, waits for them, and re-layouts  1.57 us

profile of v6, /device:TPU:1, one launch (start us, length us, event | category | flops | bytes accessed | tf_op | source)
XLA Modules:
  0.0 39.4 jit_solution(14741704853696309998)
XLA Ops:
  0.0 37.8 %shard_map.64 = f32[2,4,4096]{2,1,0:T(4,128)} custom-call(s32[1,256]{1,0:T(1,128)} %bitcast.3, f32[2,256,128]{2,1,0:T(8,128)} %qu_hbm.1, f32[2,256,128]{2,1,0:T(8,128)} %off_hbm.1, s32[256,128]{1,0:T(8,128)} %rb_hbm.1, s32[256,128]{1,0:T(8,128)} %cb_hbm.1, s32[8,128]{1,0:T(8,128)} %bitcast.2), custom_call_target="tpu_custom_call" | custom-call | tf_op jit(solution)/shard_map/pallas_call | solution.py:344
  37.8 1.6 %copy.8 = f32[2,4,4096]{2,1,0:T(4,128)} copy(f32[2,4,4096]{2,1,0:T(4,128)} %shard_map.64) | data formatting | bytes 262144

commit v7 on v6

--- a/solution.py
+++ b/solution.py
@@ -38,7 +38,7 @@
 
 def spectra_kernel(bands, lons, subs, lag, unroll, target_hbm, qu_hbm, off_hbm, rb_hbm, cb_hbm, orders_hbm, out_ref,
                    target_ref, qu_ref, off_ref, rb_ref, cb_ref, orders_ref, keys_row, keys, sums, tiles, halo, order_col, t_hi, t_lo,
-                   turn, spin, g_hi, g_lo, part, arrived, total, landed, ready, in_sem, keys_sem, halo_send, halo_recv, x_send, x_recv, a_send, a_recv):
+                   turn, spin, held, g_hi, g_lo, part, arrived, total, landed, ready, in_sem, keys_sem, halo_send, halo_recv, x_send, x_recv, a_send, a_recv):
     band = lax.axis_index("band")
     lon = lax.axis_index("lon")
     run = bands // subs
@@ -153,14 +153,24 @@
     lax.fori_loop(48, 64, gather, 0, unroll=16)
     pl.semaphore_wait(barrier, len(greeted))
 
-    upward = pltpu.make_async_remote_copy(
-        src_ref=tiles.at[pl.ds(0, 16)], dst_ref=halo.at[1], send_sem=halo_send.at[0], recv_sem=halo_recv.at[1],
-        device_id=(above, lon), device_id_type=MESH)
-    downward = pltpu.make_async_remote_copy(
-        src_ref=tiles.at[pl.ds(48, 16)], dst_ref=halo.at[0], send_sem=halo_send.at[1], recv_sem=halo_recv.at[0],
-        device_id=(below, lon), device_id_type=MESH)
-    upward.start()
-    downward.start()
+    def to_band(toward, part_of):
+        return pltpu.make_async_remote_copy(
+            src_ref=tiles.at[pl.ds(48 * (1 - toward) + 8 * part_of, 8)], dst_ref=halo.at[toward, pl.ds(8 * part_of, 8)],
+            send_sem=halo_send.at[toward, part_of], recv_sem=halo_recv.at[toward, part_of],
+            device_id=(above if toward else below, lon), device_id_type=MESH)
+
+    even = lax.rem(band, 2) == 0
+    for part_of in (1, 0):
+        @pl.when(even)
+        def _():
+            to_band(1, part_of).start()
+            to_band(0, part_of).start()
+
+        @pl.when(jnp.logical_not(even))
+        def _():
+            to_band(0, part_of).start()
+            to_band(1, part_of).start()
+
     for step in range(1, width):
         pl.semaphore_signal(ready, inc=1, device_id=(in_row(step), lon), device_id_type=MESH)
 
@@ -175,7 +185,7 @@
     _, sine = cos_sin((cycle.astype(jnp.float32) + 0.5) * (1.0 / 2048))
     weight = sine * (math.pi * math.sqrt(2.0 / (bands * ROWS_DEV * NPHI)))
     low_columns = lane.astype(jnp.float32) * (1.0 / 2048)
-    spin_phase = (half * 1024 + lon * 2048).astype(jnp.float32) * (1.0 / 2048)
+    spin_phase = (half * 256 + lon * 2048).astype(jnp.float32) * (1.0 / 2048)
 
     def table(step, carry):
         group = step // lons
@@ -193,50 +203,63 @@
             t_lo[group, rows, cols] = c_lo
             t_hi[group, sine_rows, cols] = s_hi
             t_lo[group, sine_rows, cols] = s_lo
-        c, s = cos_sin(m * (256.0 / 2048))
+        c, s = cos_sin(m * (512.0 / 2048))
         turn[group, 0, rows, :] = c
         turn[group, 1, rows, :] = -s
-        eighth = (m.astype(jnp.int32) & 7).astype(jnp.float32)
-        c, s = cos_sin(eighth * spin_phase)
+        least = (m.astype(jnp.int32) & 31).astype(jnp.float32)
+        c, s = cos_sin(least * spin_phase)
         spin[group, 0, rows, :] = c * weight
         spin[group, 1, rows, :] = -s * weight
         return carry
 
     lax.fori_loop(0, subs * lons, table, 0)
 
-    upward.wait_recv()
-    downward.wait_recv()
-
-    for v in range(4):
-        for k in range(2):
-            pieces = []
-            for h in range(2):
-                for tr in range(2):
-                    tile = 2 * (v + 4 * h) + k
-                    pieces.append(tiles[16 * (tr + 1) + tile] + halo[tr, tile])
-            hi, lo = split(jnp.transpose(jnp.concatenate(pieces, 0)))
-            g_hi[pl.ds(k * 128, 128), pl.ds(v * 128, 128)] = hi
-            g_lo[pl.ds(k * 128, 128), pl.ds(v * 128, 128)] = lo
-
-    is_real = lane < 64
-
-    def transform(group):
-        def product(v):
-            cols = pl.ds(v * 128, 256)
-            value = (jnp.dot(t_hi[group], g_hi[:, cols], preferred_element_type=jnp.float32)
-                     + jnp.dot(t_hi[group], g_lo[:, cols], preferred_element_type=jnp.float32)
-                     + jnp.dot(t_lo[group], g_hi[:, cols], preferred_element_type=jnp.float32))
-            return value[:per_group], value[per_group:]
-
+    def columns_of(part_of):
+        for toward in range(2):
+            to_band(toward, part_of).wait_recv()
+        for v in range(2 * part_of, 2 * part_of + 2):
+            for k in range(2):
+                pieces = []
+                for h in range(2):
+                    for tr in range(2):
+                        tile = 2 * (2 * v + h) + k
+                        pieces.append(tiles[16 * (tr + 1) + tile] + halo[tr, tile])
+                hi, lo = split(jnp.transpose(jnp.concatenate(pieces, 0)))
+                g_hi[pl.ds(k * 128, 128), pl.ds(v * 128, 128)] = hi
+                g_lo[pl.ds(k * 128, 128), pl.ds(v * 128, 128)] = lo
+
+    def product(group, part_of):
+        cols = pl.ds(part_of * 256, 256)
+        value = (jnp.dot(t_hi[group], g_hi[:, cols], preferred_element_type=jnp.float32)
+                 + jnp.dot(t_hi[group], g_lo[:, cols], preferred_element_type=jnp.float32)
+                 + jnp.dot(t_lo[group], g_hi[:, cols], preferred_element_type=jnp.float32))
+        return value[:per_group], value[per_group:]
+
+    columns_of(1)
+
+    def begin(group, carry):
+        c, s = product(group, 1)
         wr = turn[group, 0]
         wi = turn[group, 1]
-        re = im = None
-        for v in (2, 0):
-            c, s = product(v)
-            for side in (1, 0):
-                c1 = c[:, side * 128:side * 128 + 128]
-                s1 = s[:, side * 128:side * 128 + 128]
-                re, im = (c1, s1) if re is None else (re * wr - im * wi + c1, re * wi + im * wr + s1)
+        re, im = c[:, 128:], s[:, 128:]
+        held[group, 0] = re * wr - im * wi + c[:, :128]
+        held[group, 1] = re * wi + im * wr + s[:, :128]
+        return carry
+
+    lax.fori_loop(0, subs, begin, 0)
+    columns_of(0)
+
+    is_real = lane < 64
+
+    def transform(group):
+        c, s = product(group, 0)
+        wr = turn[group, 0]
+        wi = turn[group, 1]
+        re, im = held[group, 0], held[group, 1]
+        for side in (1, 0):
+            c1 = c[:, side * 128:side * 128 + 128]
+            s1 = s[:, side * 128:side * 128 + 128]
+            re, im = re * wr - im * wi + c1, re * wi + im * wr + s1
         pr = spin[group, 0]
         pi = spin[group, 1]
         zr = re * pr - im * pi
@@ -328,8 +351,9 @@
                 for j in range(bands // 4):
                     out_ref[i, pl.ds(2 * f + reim, 1), pl.ds(j * 128, 128)] = value[j:j + 1, :]
 
-    upward.wait_send()
-    downward.wait_send()
+    for part_of in range(2):
+        for toward in range(2):
+            to_band(toward, part_of).wait_send()
     for sub in range(subs):
         for step in range(1, lons):
             over_lon(step, group_of(sub), sub).wait_send()
@@ -363,6 +387,7 @@
             pltpu.VMEM((subs, 512, 256), bf16),
             pltpu.VMEM((subs, 2, 256, 128), f32),
             pltpu.VMEM((subs, 2, 256, 128), f32),
+            pltpu.VMEM((subs, 2, 256, 128), f32),
             pltpu.VMEM((256, 512), bf16),
             pltpu.VMEM((256, 512), bf16),
             pltpu.VMEM((subs, lons, 256 // subs, 128), f32),
@@ -372,8 +397,8 @@
             pltpu.SemaphoreType.REGULAR,
             pltpu.SemaphoreType.DMA((6,)),
             pltpu.SemaphoreType.DMA,
-            pltpu.SemaphoreType.DMA((2,)),
-            pltpu.SemaphoreType.DMA((2,)),
+            pltpu.SemaphoreType.DMA((2, 2)),
+            pltpu.SemaphoreType.DMA((2, 2)),
             pltpu.SemaphoreType.DMA((lons, subs)),
             pltpu.SemaphoreType.DMA((lons, subs)),
             pltpu.SemaphoreType.DMA,

time: 39.5 us -> 40.6 us (1.028)
  Pallas kernels: 37.8 us -> 38.9 us
    pallas_call x1, Pallas kernels: 37.8 us -> 38.9 us  [spectra(): pl.pallas_call(functools.partial(spectra_kernel, bands, lons, subs, lag,...]
where the time goes in v7:
time: 40.6 us; the launch traced here: 40.5 us
  Pallas kernels  38.9 us (96%)
  local copies, waits for them, and re-layouts  1.57 us (4%)
    pallas_call x1, Pallas kernels, spectra(): pl.pallas_call(functools.partial(spectra_kernel, bands, lons, subs, lag,...  38.9 us
    unnamed x1, local copies, waits for them, and re-layouts  1.57 us

profile of v7, /device:TPU:1, one launch (start us, length us, event | category | flops | bytes accessed | tf_op | source)
XLA Modules:
  0.0 40.5 jit_solution(7272100370747649257)
XLA Ops:
  0.0 38.9 %shard_map.64 = f32[2,4,4096]{2,1,0:T(4,128)} custom-call(s32[1,256]{1,0:T(1,128)} %bitcast.3, f32[2,256,128]{2,1,0:T(8,128)} %qu_hbm.1, f32[2,256,128]{2,1,0:T(8,128)} %off_hbm.1, s32[256,128]{1,0:T(8,128)} %rb_hbm.1, s32[256,128]{1,0:T(8,128)} %cb_hbm.1, s32[8,128]{1,0:T(8,128)} %bitcast.2), custom_call_target="tpu_custom_call" | custom-call | tf_op jit(solution)/shard_map/pallas_call | solution.py:368
  38.9 1.6 %copy.8 = f32[2,4,4096]{2,1,0:T(4,128)} copy(f32[2,4,4096]{2,1,0:T(4,128)} %shard_map.64) | data formatting | bytes 262144

commit v8 on v6

--- a/solution.py
+++ b/solution.py
@@ -37,8 +37,8 @@
 
 
 def spectra_kernel(bands, lons, subs, lag, unroll, target_hbm, qu_hbm, off_hbm, rb_hbm, cb_hbm, orders_hbm, out_ref,
-                   target_ref, qu_ref, off_ref, rb_ref, cb_ref, orders_ref, keys_row, keys, sums, tiles, halo, order_col, t_hi, t_lo,
-                   turn, spin, g_hi, g_lo, part, arrived, total, landed, ready, in_sem, keys_sem, halo_send, halo_recv, x_send, x_recv, a_send, a_recv):
+                   target_ref, qu_ref, off_ref, rb_ref, cb_ref, orders_ref, keys_row, keys, sums, tiles, halo, order_col, trig,
+                   turn, spin, folded, part, arrived, total, landed, ready, in_sem, keys_sem, halo_send, halo_recv, x_send, x_recv, a_send, a_recv):
     band = lax.axis_index("band")
     lon = lax.axis_index("lon")
     run = bands // subs
@@ -174,7 +174,7 @@
     cycle = band * ROWS_DEV + ((lane // 32) % 2) * TR + lane % 16
     _, sine = cos_sin((cycle.astype(jnp.float32) + 0.5) * (1.0 / 2048))
     weight = sine * (math.pi * math.sqrt(2.0 / (bands * ROWS_DEV * NPHI)))
-    low_columns = lane.astype(jnp.float32) * (1.0 / 2048)
+    half_columns = (lane.astype(jnp.float32) + 0.5) * (1.0 / 2048)
     spin_phase = (half * 1024 + lon * 2048).astype(jnp.float32) * (1.0 / 2048)
 
     def table(step, carry):
@@ -183,21 +183,17 @@
         first = group * per_group + 2 * ell
         m = jnp.concatenate([order_col[pl.ds(first + place, run, stride=2 * lons), :] for place in range(2)], 0)
         rows = pl.ds(pl.multiple_of(ell * 2 * run, 2 * run), 2 * run)
-        sine_rows = pl.ds(pl.multiple_of(per_group + ell * 2 * run, 2 * run), 2 * run)
-        for side in range(2):
-            c, s = cos_sin(m * (low_columns + side * (128.0 / 2048)))
-            c_hi, c_lo = split(c)
-            s_hi, s_lo = split(-s)
-            cols = pl.ds(side * 128, 128)
-            t_hi[group, rows, cols] = c_hi
-            t_lo[group, rows, cols] = c_lo
-            t_hi[group, sine_rows, cols] = s_hi
-            t_lo[group, sine_rows, cols] = s_lo
+        low_rows = pl.ds(pl.multiple_of(per_group + ell * 2 * run, 2 * run), 2 * run)
+        c, s = cos_sin(m * half_columns)
+        for q, value in enumerate((c, -s)):
+            hi, lo = split(value)
+            trig[group, q, rows, :] = jnp.concatenate([hi, hi], 1)
+            trig[group, q, low_rows, :] = jnp.concatenate([lo, lo], 1)
         c, s = cos_sin(m * (256.0 / 2048))
         turn[group, 0, rows, :] = c
         turn[group, 1, rows, :] = -s
         eighth = (m.astype(jnp.int32) & 7).astype(jnp.float32)
-        c, s = cos_sin(eighth * spin_phase)
+        c, s = cos_sin(eighth * spin_phase + m * (127.5 / 2048))
         spin[group, 0, rows, :] = c * weight
         spin[group, 1, rows, :] = -s * weight
         return carry
@@ -207,32 +203,39 @@
     upward.wait_recv()
     downward.wait_recv()
 
-    for v in range(4):
-        for k in range(2):
+    sides = []
+    for k in range(2):
+        columns = []
+        for v in range(4):
             pieces = []
             for h in range(2):
                 for tr in range(2):
                     tile = 2 * (v + 4 * h) + k
                     pieces.append(tiles[16 * (tr + 1) + tile] + halo[tr, tile])
-            hi, lo = split(jnp.transpose(jnp.concatenate(pieces, 0)))
-            g_hi[pl.ds(k * 128, 128), pl.ds(v * 128, 128)] = hi
-            g_lo[pl.ds(k * 128, 128), pl.ds(v * 128, 128)] = lo
+            columns.append(jnp.transpose(jnp.concatenate(pieces, 0)))
+        sides.append(jnp.concatenate(columns, 1))
+    flip = (lax.broadcasted_iota(jnp.int32, (128, 128), 0) + lax.broadcasted_iota(jnp.int32, (128, 128), 1)) == 127
+    flip = jnp.where(flip, 1.0, 0.0).astype(jnp.bfloat16)
+    hi, lo = split(sides[0])
+    turned = (jnp.dot(flip, hi, preferred_element_type=jnp.float32)
+              + jnp.dot(flip, lo, preferred_element_type=jnp.float32))
+    for q, value in enumerate((sides[1] + turned, sides[1] - turned)):
+        hi, lo = split(value)
+        folded[q, pl.ds(0, 128), :] = hi
+        folded[q, pl.ds(128, 128), :] = lo
 
     is_real = lane < 64
 
     def transform(group):
-        def product(v):
-            cols = pl.ds(v * 128, 256)
-            value = (jnp.dot(t_hi[group], g_hi[:, cols], preferred_element_type=jnp.float32)
-                     + jnp.dot(t_hi[group], g_lo[:, cols], preferred_element_type=jnp.float32)
-                     + jnp.dot(t_lo[group], g_hi[:, cols], preferred_element_type=jnp.float32))
-            return value[:per_group], value[per_group:]
+        def product(v, q):
+            value = jnp.dot(trig[group, q], folded[q, :, pl.ds(v * 128, 256)], preferred_element_type=jnp.float32)
+            return value[:per_group] + value[per_group:]
 
         wr = turn[group, 0]
         wi = turn[group, 1]
         re = im = None
         for v in (2, 0):
-            c, s = product(v)
+            c, s = product(v, 0), product(v, 1)
             for side in (1, 0):
                 c1 = c[:, side * 128:side * 128 + 128]
                 s1 = s[:, side * 128:side * 128 + 128]
@@ -359,12 +362,10 @@
             pltpu.VMEM((64, 2 * TR, TC), f32),
             pltpu.VMEM((2, 16, 2 * TR, TC), f32),
             pltpu.VMEM((1024, 128), f32),
-            pltpu.VMEM((subs, 512, 256), bf16),
-            pltpu.VMEM((subs, 512, 256), bf16),
+            pltpu.VMEM((subs, 2, 512, 256), bf16),
             pltpu.VMEM((subs, 2, 256, 128), f32),
             pltpu.VMEM((subs, 2, 256, 128), f32),
-            pltpu.VMEM((256, 512), bf16),
-            pltpu.VMEM((256, 512), bf16),
+            pltpu.VMEM((2, 256, 512), bf16),
             pltpu.VMEM((subs, lons, 256 // subs, 128), f32),
             pltpu.VMEM((subs, lons, 256 // subs, 128), f32),
             pltpu.VMEM((256, 128), f32),

time: 39.5 us -> 39.3 us (level)
  no operation moved by 1% of the time
where the time goes in v8:
time: 39.3 us; the launch traced here: 39.2 us
  Pallas kernels  37.6 us (96%)
  local copies, waits for them, and re-layouts  1.57 us (4%)
    pallas_call x1, Pallas kernels, spectra(): pl.pallas_call(functools.partial(spectra_kernel, bands, lons, subs, lag,...  37.6 us
    unnamed x1, local copies, waits for them, and re-layouts  1.57 us

profile of v8, /device:TPU:1, one launch (start us, length us, event | category | flops | bytes accessed | tf_op | source)
XLA Modules:
  0.0 39.2 jit_solution(16103677077222299247)
XLA Ops:
  0.0 37.6 %shard_map.64 = f32[2,4,4096]{2,1,0:T(4,128)} custom-call(s32[1,256]{1,0:T(1,128)} %bitcast.3, f32[2,256,128]{2,1,0:T(8,128)} %qu_hbm.1, f32[2,256,128]{2,1,0:T(8,128)} %off_hbm.1, s32[256,128]{1,0:T(8,128)} %rb_hbm.1, s32[256,128]{1,0:T(8,128)} %cb_hbm.1, s32[8,128]{1,0:T(8,128)} %bitcast.2), custom_call_target="tpu_custom_call" | custom-call | tf_op jit(solution)/shard_map/pallas_call | solution.py:347
  37.6 1.6 %copy.8 = f32[2,4,4096]{2,1,0:T(4,128)} copy(f32[2,4,4096]{2,1,0:T(4,128)} %shard_map.64) | data formatting | bytes 262144

commit v9 on v8

--- a/solution.py
+++ b/solution.py
@@ -340,7 +340,7 @@
     pltpu.make_async_copy(total.at[others], total.at[others], a_send).wait()
 
 
-def spectra(targets, qu, off, rb, cb, orders, bands, lons, subs=4, lag=3, unroll=64):
+def spectra(targets, qu, off, rb, cb, orders, bands, lons, subs=4, lag=3, unroll=128):
     V = pl.BlockSpec(memory_space=pltpu.VMEM)
     f32, bf16 = jnp.float32, jnp.bfloat16
     blocks = rb.shape[0]

time: 39.3 us -> 38.7 us (0.985)
  Pallas kernels: 37.6 us -> 37 us
    pallas_call x1, Pallas kernels: 37.6 us -> 37 us  [spectra(): pl.pallas_call(functools.partial(spectra_kernel, bands, lons, subs, lag,...]
where the time goes in v9:
time: 38.7 us; the launch traced here: 38.6 us
  Pallas kernels  37 us (96%)
  local copies, waits for them, and re-layouts  1.57 us (4%)
    pallas_call x1, Pallas kernels, spectra(): pl.pallas_call(functools.partial(spectra_kernel, bands, lons, subs, lag,...  37 us
    unnamed x1, local copies, waits for them, and re-layouts  1.57 us

profile of v9, /device:TPU:1, one launch (start us, length us, event | category | flops | bytes accessed | tf_op | source)
XLA Modules:
  0.0 38.6 jit_solution(10906289731449809184)
XLA Ops:
  0.0 37.0 %shard_map.64 = f32[2,4,4096]{2,1,0:T(4,128)} custom-call(s32[1,256]{1,0:T(1,128)} %bitcast.3, f32[2,256,128]{2,1,0:T(8,128)} %qu_hbm.1, f32[2,256,128]{2,1,0:T(8,128)} %off_hbm.1, s32[256,128]{1,0:T(8,128)} %rb_hbm.1, s32[256,128]{1,0:T(8,128)} %cb_hbm.1, s32[8,128]{1,0:T(8,128)} %bitcast.2), custom_call_target="tpu_custom_call" | custom-call | tf_op jit(solution)/shard_map/pallas_call | solution.py:347
  37.0 1.6 %copy.8 = f32[2,4,4096]{2,1,0:T(4,128)} copy(f32[2,4,4096]{2,1,0:T(4,128)} %shard_map.64) | data formatting | bytes 262144

commit v10 on v9

--- a/solution.py
+++ b/solution.py
@@ -340,7 +340,7 @@
     pltpu.make_async_copy(total.at[others], total.at[others], a_send).wait()
 
 
-def spectra(targets, qu, off, rb, cb, orders, bands, lons, subs=4, lag=3, unroll=128):
+def spectra(targets, qu, off, rb, cb, orders, bands, lons, subs=4, lag=3, unroll=256):
     V = pl.BlockSpec(memory_space=pltpu.VMEM)
     f32, bf16 = jnp.float32, jnp.bfloat16
     blocks = rb.shape[0]

time: 38.7 us -> 38.4 us (level)
  no operation moved by 1% of the time
where the time goes in v10:
time: 38.4 us; the launch traced here: 38.3 us
  Pallas kernels  36.7 us (96%)
  local copies, waits for them, and re-layouts  1.57 us (4%)
    pallas_call x1, Pallas kernels, spectra(): pl.pallas_call(functools.partial(spectra_kernel, bands, lons, subs, lag,...  36.7 us
    unnamed x1, local copies, waits for them, and re-layouts  1.57 us

profile of v10, /device:TPU:1, one launch (start us, length us, event | category | flops | bytes accessed | tf_op | source)
XLA Modules:
  0.0 38.3 jit_solution(5494204870126856382)
XLA Ops:
  0.0 36.7 %shard_map.64 = f32[2,4,4096]{2,1,0:T(4,128)} custom-call(s32[1,256]{1,0:T(1,128)} %bitcast.3, f32[2,256,128]{2,1,0:T(8,128)} %qu_hbm.1, f32[2,256,128]{2,1,0:T(8,128)} %off_hbm.1, s32[256,128]{1,0:T(8,128)} %rb_hbm.1, s32[256,128]{1,0:T(8,128)} %cb_hbm.1, s32[8,128]{1,0:T(8,128)} %bitcast.2), custom_call_target="tpu_custom_call" | custom-call | tf_op jit(solution)/shard_map/pallas_call | solution.py:347
  36.7 1.6 %copy.8 = f32[2,4,4096]{2,1,0:T(4,128)} copy(f32[2,4,4096]{2,1,0:T(4,128)} %shard_map.64) | data formatting | bytes 262144
